TPU v7x, 256 devices: a whole 4x4x8 slice. The times are simulated.
256 devices in a mesh: dp: 8 (over z_hi, x), expert: 32 (over z_lo, y, core).
Axes of the slice: x: 4, y: 4, z: 8 (z_hi: 2, z_lo: 4; z = z_hi * 4 + z_lo), core: 2. Of those that a mesh axis runs over, the one named last changes fastest.
Arguments:
- tokens: bfloat16 [32768, 1792], P(('dp', 'expert')), may hold values from -6 to 6
- routes: int32 [32768, 4], P(('dp', 'expert')), may hold values from 0 to 31, all different within a row; in each aligned block of 128 rows (0 to 127, 128 to 255, ...) at most 32 rows name the same one
- route_weight: float32 [32768, 4], P(('dp', 'expert')), may hold values from 0.1 to 1
- w_in: float32 [32, 2, 1792, 1280], P('expert', None, 'dp'), may hold values from -0.125 to 0.125
- m_in: float32 [32, 2, 1792, 1280], P('expert', None, 'dp'), may hold values from -6 to 6
- v_in: float32 [32, 2, 1792, 1280], P('expert', None, 'dp'), may hold values from 0.5 to 20
- g_in: bfloat16 [32, 2, 1792, 1280], P('expert', None, 'dp'), may hold values from -30 to 30
- w_out: float32 [32, 1280, 1792], P('expert', 'dp'), may hold values from -0.15625 to 0.15625
- m_out: float32 [32, 1280, 1792], P('expert', 'dp'), may hold values from -6 to 6
- v_out: float32 [32, 1280, 1792], P('expert', 'dp'), may hold values from 0.5 to 20
- g_out: bfloat16 [32, 1280, 1792], P('expert', 'dp'), may hold values from -30 to 30
Outputs:
- mixed: bfloat16 [32768, 1792], P(('dp', 'expert'))
Inputs may be any that keep to these rules, and one draw needn't show every extreme that they name: `routes`: A token's 4 experts differ. Within the rows of one device (aligned blocks of 128 tokens) each expert is named at most 32 times, a bound that some block reaches.
All inputs are finite; a program needn't handle non-finite values.
Results may differ from a plain program's by a relative error of at most 0.008.
Values may be sent and summed in bfloat16 or wider, within the bound.
A program may use at most 128 MiB of HBM per device.

v0:
```python
import jax
import jax.numpy as jnp
from jax import lax
from jax.sharding import PartitionSpec as P

beta_one = 0.9
beta_two = 0.95
corr_one = 0.99997343860111
corr_two = 0.99407947077967
adam_eps = 1e-08
learn_rate = 0.01
weight_decay = 0.1


def adamw(master, moment, second, gradient):
    grad_value = gradient.astype(jnp.float32)
    moment_new = beta_one * moment + (1.0 - beta_one) * grad_value
    second_new = beta_two * second + (1.0 - beta_two) * grad_value * grad_value
    update = moment_new / corr_one / (jnp.sqrt(second_new / corr_two) + adam_eps)
    return (master - learn_rate * (update + weight_decay * master)).astype(jnp.bfloat16)


def expert_apply(block_rows, gate_up, down_proj):
    gate_pre = jnp.dot(block_rows, gate_up[0], preferred_element_type=jnp.float32)
    up_pre = jnp.dot(block_rows, gate_up[1], preferred_element_type=jnp.float32)
    hidden = (jax.nn.silu(gate_pre) * up_pre).astype(jnp.bfloat16)
    return jnp.dot(hidden, down_proj, preferred_element_type=jnp.float32).astype(jnp.bfloat16)


def per_device(tokens, routes, route_weight, w_in, m_in, v_in, g_in, w_out, m_out, v_out, g_out):
    groups = lax.axis_size("expert")
    tok_rows, width = tokens.shape
    top_count = routes.shape[1]
    capacity = 2 * tok_rows * top_count // groups
    slot_total = groups * capacity
    flat_routes = routes.reshape(-1)
    owners = jnp.arange(tok_rows * top_count, dtype=jnp.int32) // top_count
    onehot = (flat_routes[:, None] == jnp.arange(groups, dtype=jnp.int32)[None, :]).astype(
        jnp.int32
    )
    earlier = jnp.cumsum(onehot, axis=0) - onehot
    slot_ids = flat_routes * capacity + jnp.sum(earlier * onehot, axis=1)
    matches = (jnp.arange(slot_total, dtype=jnp.int32)[:, None] == slot_ids[None, :]).astype(
        jnp.int32
    )
    live_flags = jnp.sum(matches, axis=1)
    sources = jnp.sum(matches * owners[None, :], axis=1)
    outgoing = jnp.where(
        live_flags[:, None] > 0, jnp.take(tokens, sources, axis=0), jnp.zeros((), jnp.bfloat16)
    )
    outgoing = outgoing.reshape(groups, capacity, width)
    gate_up_own = adamw(w_in, m_in, v_in, g_in)
    down_own = adamw(w_out, m_out, v_out, g_out)
    gate_up_all, down_all = (
        lax.all_gather(gate_up_own, "dp", axis=2, tiled=True),
        lax.all_gather(down_own, "dp", axis=1, tiled=True),
    )
    gate_up_all = gate_up_all[0]
    down_all = down_all[0]
    arrived = lax.all_to_all(outgoing, "expert", split_axis=0, concat_axis=0, tiled=True)
    src_count, item_count, depth = arrived.shape
    results = expert_apply(arrived.reshape(src_count * item_count, depth), gate_up_all, down_all)
    returned = lax.all_to_all(
        results.reshape(src_count, item_count, depth),
        "expert",
        split_axis=0,
        concat_axis=0,
        tiled=True,
    )
    back_rows = returned.reshape(slot_total, width)
    picked = jnp.take(back_rows, slot_ids, axis=0).reshape(tok_rows, top_count, width)
    mixed = jnp.einsum("tkd,tk->td", picked.astype(jnp.float32), route_weight)
    return mixed.astype(jnp.bfloat16)


def solution(mesh):
    placed = (
        P(("dp", "expert"), None),
        P(("dp", "expert"), None),
        P(("dp", "expert"), None),
        P("expert", None, "dp", None),
        P("expert", None, "dp", None),
        P("expert", None, "dp", None),
        P("expert", None, "dp", None),
        P("expert", "dp", None),
        P("expert", "dp", None),
        P("expert", "dp", None),
        P("expert", "dp", None),
    )
    return jax.shard_map(
        per_device, mesh=mesh, in_specs=placed, out_specs=P(("dp", "expert"), None), check_vma=False
    )
```

profile of v0, /device:TPU:32, one launch (start us, length us, event | category | flops | bytes accessed | tf_op | source)
XLA Modules:
  0.0 468.0 jit_solution(3594123796976531903)
XLA Ops:
  6.5 6.3 %fusion.16 = bf16[1,2,224,1280]{3,2,1,0:T(8,128)(2,1)} fusion(f32[1,2,224,1280]{3,2,1,0:T(8,128)} %param.14, f32[1,2,224,1280]{3,2,1,0:T(8,128)} %param.16, bf16[1,2,224,1280]{3,2,1,0:T(8,128)(2,1)} %param.17, f32[1,2,224,1280]{3,2,1,0:T(8,128)} %param.15), kind=kLoop, calls=%fused_computation.22 | loop fusion | flops 9748480 | bytes 9175040 | tf_op jit(solution)/shard_map/convert_element_type | solution.py:20
  12.9 0.1 copy.21
  13.3 1.2 reduce-window.6
  14.4 0.2 slice_reduce_fusion
  14.7 0.1 fusion.34
  14.8 0.6 convert_reduce_fusion
  15.7 5.8 %gather_fusion = bf16[1024,1792]{1,0:T(8,128)(2,1)} fusion(bf16[128,1792]{1,0:T(8,128)(2,1)S(1)} %copy-done, s32[1024]{0:T(1024)S(1)} %broadcast_clamp_fusion), kind=kCustom, calls=%fused_computation | custom fusion | bytes 7344128 | tf_op jit(solution)/shard_map/jit(_take)/gather | solution.py:49
  21.5 3.6 select_select_fusion
  25.1 9.1 %all-to-all-start = ((bf16[32,32,1792]{2,1,0:T(8,128)(2,1)}), bf16[32,32,1792]{2,1,0:T(8,128)(2,1)}, u32[]{:S(2)}, u32[]{:S(2)}) async-start(bf16[32,32,1792]{2,1,0:T(8,128)(2,1)} %select_select_fusion), calls=%async_computation | async-start | bytes 7340032 | tf_op jit(solution)/shard_map/all_to_all | solution.py:60
  34.3 0.2 all-gather.5.cloned.1.call-start
  34.5 3.0 fusion.30
  37.5 195.5 %all-to-all-done = bf16[32,32,1792]{2,1,0:T(8,128)(2,1)} async-done(((bf16[32,32,1792]{2,1,0:T(8,128)(2,1)}), bf16[32,32,1792]{2,1,0:T(8,128)(2,1)}, u32[]{:S(2)}, u32[]{:S(2)}) %all-to-all-start) | async-done | bytes 3670048 | tf_op jit(solution)/shard_map/all_to_all | solution.py:60
  233.1 10.7 %fusion = f32[1024,1280]{1,0:T(8,128)} fusion(bf16[1024,1792]{1,0:T(8,128)(2,1)} %bitcast.4, bf16[1,2,1792,1280]{3,2,1,0:T(8,128)(2,1)} %all-gather.3.cloned.1.call-done), kind=kOutput, calls=%fused_computation.5 | convolution fusion | flops 4697620480 | bytes 13500416 | tf_op jit(solution)/shard_map/dot_general | solution.py:24
  243.8 103.7 %all-gather.5.cloned.1.call-done = bf16[1,1280,1792]{2,1,0:T(8,128)(2,1)} async-done(((bf16[1,160,1792]{2,1,0:T(8,128)(2,1)}), bf16[1,1280,1792]{2,1,0:T(8,128)(2,1)}) %all-gather.5.cloned.1.call-update) | async-done | bytes 4587536 | tf_op jit(solution)/shard_map/all_gather | solution.py:56
  347.5 16.4 %fusion.3 = bf16[1024,1792]{1,0:T(8,128)(2,1)} fusion(bf16[1,1280,1792]{2,1,0:T(8,128)(2,1)} %all-gather.5.cloned.1.call-done, f32[1024,1280]{1,0:T(8,128)} %fusion, bf16[1024,1792]{1,0:T(8,128)(2,1)} %bitcast.4, bf16[1,2,1792,1280]{3,2,1,0:T(8,128)(2,1)} %all-gather.3.cloned.1.call-done), kind=kOutput, calls=%fused_computation.8 | convolution fusion | flops 9404940288 | bytes 21757952 | tf_op jit(solution)/shard_map/dot_general | solution.py:27
  363.8 6.1 %all-to-all-start.1 = ((bf16[32,32,1792]{2,1,0:T(8,128)(2,1)}), bf16[32,32,1792]{2,1,0:T(8,128)(2,1)}, u32[]{:S(2)}, u32[]{:S(2)}) async-start(bf16[32,32,1792]{2,1,0:T(8,128)(2,1)} %bitcast.48), calls=%async_computation.1 | async-start | bytes 7340032 | tf_op jit(solution)/shard_map/all_to_all | solution.py:63
  370.1 0.1 copy.26
  370.4 0.1 copy.25
  370.5 0.2 copy.27
  370.7 79.0 %all-to-all-done.1 = bf16[32,32,1792]{2,1,0:T(8,128)(2,1)} async-done(((bf16[32,32,1792]{2,1,0:T(8,128)(2,1)}), bf16[32,32,1792]{2,1,0:T(8,128)(2,1)}, u32[]{:S(2)}, u32[]{:S(2)}) %all-to-all-start.1) | async-done | bytes 3670048 | tf_op jit(solution)/shard_map/all_to_all | solution.py:63
  449.7 6.5 %gather_fusion.1 = bf16[512,1792]{1,0:T(8,128)(2,1)S(1)} fusion(bf16[1024,1792]{1,0:T(8,128)(2,1)} %bitcast.9, s32[1024]{0:T(1024)S(1)} %pad_clamp_fusion), kind=kCustom, calls=%fused_computation.1 | custom fusion | bytes 3672064 | tf_op jit(solution)/shard_map/jit(_take)/gather | solution.py:71
  456.1 1.5 gather.15
  457.6 2.7 fusion.17
  460.3 0.8 copy.32
  (35 shorter events, 0.8 us)
Async XLA Ops:
  6.5 9.1 %copy-start = (bf16[128,1792]{1,0:T(8,128)(2,1)S(1)}, bf16[128,1792]{1,0:T(8,128)(2,1)}, u32[]{:S(2)}) copy-start(bf16[128,1792]{1,0:T(8,128)(2,1)} %param.11) | copy-start | bytes 1376260
  6.5 6.4 %copy-start.4 = (s32[128,4]{0,1:T(4,128)S(1)}, s32[128,4]{0,1:T(4,128)}, u32[]{:S(2)}) copy-start(s32[128,4]{0,1:T(4,128)} %param.12) | copy-start | bytes 6148
  6.5 226.5 %all-gather.3.cloned.1.call-start = ((), (), s32[]{:S(2)}) async-start(), calls=%async_computation.2 | async-start | bytes 10321920 | tf_op jit(solution)/shard_map/all_gather | solution.py:55
  25.1 9.4 %copy-start.1 = (f32[1,160,1792]{2,1,0:T(8,128)S(1)}, f32[1,160,1792]{2,1,0:T(8,128)}, u32[]{:S(2)}) copy-start(f32[1,160,1792]{2,1,0:T(8,128)} %param.18) | copy-start | bytes 3440644
  25.1 9.4 %copy-start.2 = (f32[1,160,1792]{2,1,0:T(8,128)S(1)}, f32[1,160,1792]{2,1,0:T(8,128)}, u32[]{:S(2)}) copy-start(f32[1,160,1792]{2,1,0:T(8,128)} %param.20) | copy-start | bytes 3440644
  25.1 9.4 %copy-start.3 = (bf16[1,160,1792]{2,1,0:T(8,128)(2,1)S(1)}, bf16[1,160,1792]{2,1,0:T(8,128)(2,1)}, u32[]{:S(2)}) copy-start(bf16[1,160,1792]{2,1,0:T(8,128)(2,1)} %param.21) | copy-start | bytes 1720324
  25.1 207.9 %all-to-all-start = ((bf16[32,32,1792]{2,1,0:T(8,128)(2,1)}), bf16[32,32,1792]{2,1,0:T(8,128)(2,1)}, u32[]{:S(2)}, u32[]{:S(2)}) async-start(bf16[32,32,1792]{2,1,0:T(8,128)(2,1)} %select_select_fusion), calls=%async_computation | async-start | bytes 7340032 | tf_op jit(solution)/shard_map/all_to_all | solution.py:60
  34.3 313.2 %all-gather.5.cloned.1.call-start = ((), (), s32[]{:S(2)}) async-start(), calls=%async_computation.3 | async-start | bytes 5160960 | tf_op jit(solution)/shard_map/all_gather | solution.py:56
  363.8 6.7 %copy-start.5 = (f32[128,4]{0,1:T(4,128)S(1)}, f32[128,4]{0,1:T(4,128)}, u32[]{:S(2)}) copy-start(f32[128,4]{0,1:T(4,128)} %param.13) | copy-start | bytes 6148
  363.8 85.8 %all-to-all-start.1 = ((bf16[32,32,1792]{2,1,0:T(8,128)(2,1)}), bf16[32,32,1792]{2,1,0:T(8,128)(2,1)}, u32[]{:S(2)}, u32[]{:S(2)}) async-start(bf16[32,32,1792]{2,1,0:T(8,128)(2,1)} %bitcast.48), calls=%async_computation.1 | async-start | bytes 7340032 | tf_op jit(solution)/shard_map/all_to_all | solution.py:63
Sparse Core Ops, SparseCore 0:
  13.0 160.6 all-gather.2
  176.3 171.0 all-gather.4
where the time goes:
time: 472 us; the launch traced here: 468 us
  waiting for transfers between devices  378 us (80%)
  matrix products  29.8 us (6%)
  local copies, waits for them, and re-layouts  16 us (3%)
  starting transfers between devices  15.4 us (3%)
  other arithmetic  15 us (3%)
  between operations  13.6 us (3%)
    all_to_all x1, waiting for transfers between devices, per_device(): lax.all_to_all(outgoing, 'expert', split_axis=0, concat_axis=0, tiled=True)  196 us
    all_gather x1, waiting for transfers between devices, per_device(): lax.all_gather(down_own, 'dp', axis=1, tiled=True)  104 us
    all_to_all x1, waiting for transfers between devices, per_device(): lax.all_to_all(results.reshape(src_count, item_count, depth), 'expert', s...  79 us
    dot_general x1, matrix products, expert_apply(): jnp.dot(hidden, down_proj, preferred_element_type=jnp.float32)  16.4 us
    dot_general x1, matrix products, expert_apply(): jnp.dot(block_rows, gate_up[0], preferred_element_type=jnp.float32)  10.7 us
  transfers between devices with their start and end apart: 4, of which 3 were waited for; matrix products, arithmetic and copies ran while one was open for 6% of the time, Pallas kernels for 0%

commit v1 on v0

v1 whole, which is shorter than its diff:
```python
import functools

import jax
import jax.numpy as jnp
from jax import lax
from jax.experimental import pallas as pl
from jax.experimental.pallas import tpu as pltpu
from jax.sharding import PartitionSpec as P

MESH = pl.DeviceIdType.MESH
beta_one = 0.9
beta_two = 0.95
corr_one = 0.99997343860111
corr_two = 0.99407947077967
adam_eps = 1e-08
learn_rate = 0.01
weight_decay = 0.1
XN, YN, ZN = 4, 4, 4
HALVES = 6


def adamw(master, moment, second, gradient):
    grad_value = gradient.astype(jnp.float32)
    moment_new = beta_one * moment + (1.0 - beta_one) * grad_value
    second_new = beta_two * second + (1.0 - beta_two) * grad_value * grad_value
    update = moment_new / corr_one / (jnp.sqrt(second_new / corr_two) + adam_eps)
    return (master - learn_rate * (update + weight_decay * master)).astype(jnp.bfloat16)


def gather_kernel(
    tok, w_in, m_in, v_in, g_in, w_out, m_out, v_out, g_out,
    gu_all, dn_all, tok_all,
    wi, mi, vi, gi, wo, mo, vo, go, gu_own, dn_own,
    load_sem, keep_sem, w_send, w_recv, t_send, t_recv,
):
    d, e = lax.axis_index("dp"), lax.axis_index("expert")
    zh, x = d // XN, d % XN
    z, y, c = e // (2 * YN), e // 2 % YN, e % 2
    at_dp = lambda h, i: h * XN + lax.rem(i + XN, XN)
    right, left, far = at_dp(zh, x + 1), at_dp(zh, x - 1), at_dp(zh, x + 2)
    mirror = at_dp(1 - zh, x)
    p_right, p_left, p_far = at_dp(1 - zh, x + 1), at_dp(1 - zh, x - 1), at_dp(1 - zh, x + 2)
    at_ex = lambda zz, yy, cc: lax.rem(zz + ZN, ZN) * (2 * YN) + lax.rem(yy + YN, YN) * 2 + cc

    half_in, half_out = w_in.shape[0] // 4, w_out.shape[0] // 2
    loads = []
    for h in range(HALVES):
        pairs = (
            ((w_in, wi), (m_in, mi), (v_in, vi), (g_in, gi))
            if h < 4
            else ((w_out, wo), (m_out, mo), (v_out, vo), (g_out, go))
        )
        rows = pl.ds(h * half_in, half_in) if h < 4 else pl.ds((h - 4) * half_out, half_out)
        loads.append(
            [pltpu.make_async_copy(a.at[rows], b.at[rows], load_sem.at[h, i]) for i, (a, b) in enumerate(pairs)]
        )
        for cp in loads[h]:
            cp.start()

    partners = [{"dp": right, "expert": e}, {"dp": left, "expert": e}, {"dp": mirror, "expert": e}]
    partners += [{"dp": d, "expert": at_ex(z + k, y, c)} for k in range(1, ZN)]
    partners += [{"dp": d, "expert": at_ex(z, y + k, c)} for k in range(1, YN)]
    partners += [{"dp": d, "expert": at_ex(z, y, 1 - c)}]
    barrier = pltpu.get_barrier_semaphore()
    for p in partners:
        pl.semaphore_signal(barrier, inc=1, device_id=p, device_id_type=MESH)
    pl.semaphore_wait(barrier, len(partners))

    sent = []

    def tok_copy(slot, target, op, src=None):
        return pltpu.make_async_remote_copy(
            src_ref=tok_all.at[slot] if src is None else src, dst_ref=tok_all.at[slot],
            send_sem=t_send.at[op], recv_sem=t_recv.at[op],
            device_id={"dp": d, "expert": target}, device_id_type=MESH,
        )

    TZ = lambda k: k - 1
    TY = lambda j, k: 3 + j * 3 + k - 1
    TS = lambda j, k: 15 + j * 4 + k

    def tok_send(slot, target, op, src=None):
        cp = tok_copy(slot, target, op, src)
        cp.start()
        sent.append(cp)

    def tok_wait(slot, op):
        tok_copy(slot, at_ex(z, y, 1 - c), op).wait_recv()

    own_tok = pltpu.make_async_copy(tok, tok_all.at[e], keep_sem.at[0])
    own_tok.start()
    for k in (1, 3, 2):
        tok_send(e, at_ex(z + k, y, c), TZ(k), tok)
    for k in (1, 3, 2):
        tok_send(e, at_ex(z, y + k, c), TY(0, k), tok)
    tok_send(e, at_ex(z, y, 1 - c), TS(0, 0), tok)

    def tok_z(j):
        slot = at_ex(z - j, y, c)
        tok_wait(slot, TZ(j))
        for k in (1, 3, 2):
            tok_send(slot, at_ex(z, y + k, c), TY(j, k))
        tok_send(slot, at_ex(z, y, 1 - c), TS(j, 0))

    def tok_y(j, k):
        slot = at_ex(z - j, y - k, c)
        tok_wait(slot, TY(j, k))
        tok_send(slot, at_ex(z, y, 1 - c), TS(j, k))

    def slot_of(h, owner):
        if h < 4:
            return gu_all.at[h // 2, owner, pl.ds(h % 2 * half_in, half_in)]
        return dn_all.at[owner, pl.ds((h - 4) * half_out, half_out)]

    def own_of(h):
        return gu_own.at[pl.ds(h * half_in, half_in)] if h < 4 else dn_own.at[pl.ds((h - 4) * half_out, half_out)]

    def w_copy(h, owner, target, kind, src=None):
        op = kind * HALVES + h
        return pltpu.make_async_remote_copy(
            src_ref=slot_of(h, owner) if src is None else src, dst_ref=slot_of(h, owner),
            send_sem=w_send.at[op], recv_sem=w_recv.at[op],
            device_id={"dp": target, "expert": e}, device_id_type=MESH,
        )

    R_OWN, L_OWN, MIR, F_OWN, R_P, L_P, F_P = range(7)

    def w_send_to(h, owner, target, kind, src=None):
        cp = w_copy(h, owner, target, kind, src)
        cp.start()
        sent.append(cp)

    def w_wait(h, owner, kind):
        w_copy(h, owner, right, kind).wait_recv()

    keeps = [own_tok]
    for h in range(HALVES):
        for cp in loads[h]:
            cp.wait()
        a, b, v, g, out, rows, first = (
            (wi, mi, vi, gi, gu_own, half_in, h * half_in)
            if h < 4
            else (wo, mo, vo, go, dn_own, half_out, (h - 4) * half_out)
        )

        def step(i, _, a=a, b=b, v=v, g=g, out=out, first=first):
            at = pl.ds(pl.multiple_of(first + i * 16, 16), 16)
            out[at, :] = adamw(a[at, :], b[at, :], v[at, :], g[at, :])
            return 0

        lax.fori_loop(0, rows // 16, step, 0)
        w_send_to(h, d, mirror, MIR, own_of(h))
        w_send_to(h, d, right, R_OWN, own_of(h))
        w_send_to(h, d, left, L_OWN, own_of(h))
        keep = pltpu.make_async_copy(own_of(h), slot_of(h, d), keep_sem.at[1 + h])
        keep.start()
        keeps.append(keep)

    def fwd_own(h):
        w_wait(h, left, R_OWN)
        w_wait(h, right, L_OWN)
        if h % 2 == 0:
            w_send_to(h, left, right, F_OWN)
        else:
            w_send_to(h, right, left, F_OWN)

    def from_mirror(h):
        w_wait(h, mirror, MIR)
        w_send_to(h, mirror, right, R_P)
        w_send_to(h, mirror, left, L_P)

    def fwd_mirror(h):
        w_wait(h, p_left, R_P)
        w_wait(h, p_right, L_P)
        if h % 2 == 0:
            w_send_to(h, p_left, right, F_P)
        else:
            w_send_to(h, p_right, left, F_P)

    fwd_own(0)
    tok_z(1)
    fwd_own(1)
    tok_z(3)
    from_mirror(0)
    fwd_own(2)
    tok_z(2)
    fwd_own(3)
    from_mirror(1)
    fwd_own(4)
    from_mirror(2)
    fwd_own(5)
    for k in (1, 3, 2):
        tok_y(0, k)
    fwd_mirror(0)
    from_mirror(3)
    fwd_mirror(1)
    for k in (1, 3, 2):
        tok_y(1, k)
    from_mirror(4)
    fwd_mirror(2)
    for k in (1, 3, 2):
        tok_y(3, k)
    from_mirror(5)
    fwd_mirror(3)
    for k in (1, 3, 2):
        tok_y(2, k)
    fwd_mirror(4)
    fwd_mirror(5)
    for h in range(HALVES):
        w_wait(h, far, F_OWN)
        w_wait(h, p_far, F_P)
    for j in range(ZN):
        for k in range(YN):
            tok_wait(at_ex(z - j, y - k, 1 - c), TS(j, k))
    for cp in keeps:
        cp.wait()
    for cp in sent:
        cp.wait_send()


def gather_all(tokens, w_in, m_in, v_in, g_in, w_out, m_out, v_out, g_out):
    rows_in, wide = w_in.shape
    rows_out, width = w_out.shape
    groups, dps = lax.axis_size("expert"), lax.axis_size("dp")
    any_space = pl.BlockSpec(memory_space=pl.ANY)
    f32, bf16 = jnp.float32, jnp.bfloat16
    return pl.pallas_call(
        gather_kernel,
        out_shape=(
            jax.ShapeDtypeStruct((2, dps, rows_in // 2, wide), bf16),
            jax.ShapeDtypeStruct((dps, rows_out, width), bf16),
            jax.ShapeDtypeStruct((groups,) + tokens.shape, bf16),
        ),
        in_specs=[any_space] * 9,
        out_specs=(any_space,) * 3,
        scratch_shapes=[pltpu.VMEM((rows_in, wide), t) for t in (f32, f32, f32, bf16)]
        + [pltpu.VMEM((rows_out, width), t) for t in (f32, f32, f32, bf16)]
        + [pltpu.VMEM((rows_in, wide), bf16), pltpu.VMEM((rows_out, width), bf16)]
        + [
            pltpu.SemaphoreType.DMA((HALVES, 4)),
            pltpu.SemaphoreType.DMA((HALVES + 1,)),
            pltpu.SemaphoreType.DMA((7 * HALVES,)),
            pltpu.SemaphoreType.DMA((7 * HALVES,)),
            pltpu.SemaphoreType.DMA((31,)),
            pltpu.SemaphoreType.DMA((31,)),
        ],
        name="update_and_gather",
        compiler_params=pltpu.CompilerParams(
            collective_id=0, has_side_effects=True, vmem_limit_bytes=24 * 2**20
        ),
    )(tokens, w_in, m_in, v_in, g_in, w_out, m_out, v_out, g_out)


def per_device(tokens, routes, route_weight, w_in, m_in, v_in, g_in, w_out, m_out, v_out, g_out):
    groups = lax.axis_size("expert")
    mine = lax.axis_index("expert")
    tok_rows, width = tokens.shape
    top_count = routes.shape[1]
    capacity = 2 * tok_rows * top_count // groups
    two, depth, wide = w_in.shape[1:]
    gu, dn, tok_all = gather_all(
        tokens,
        *(a.reshape(two * depth, wide) for a in (w_in, m_in, v_in, g_in)),
        *(a.reshape(a.shape[1:]) for a in (w_out, m_out, v_out, g_out)),
    )
    gate_up = gu.reshape(two, -1, wide)
    down = dn.reshape(-1, width)
    routes_t = routes.T
    routes_all = lax.all_gather(routes_t, "expert", axis=0)
    upper = (
        jnp.arange(tok_rows)[:, None] < jnp.arange(tok_rows)[None, :]
    ).astype(jnp.bfloat16)

    def ranks(hit):
        return jnp.dot(hit.astype(jnp.bfloat16), upper, preferred_element_type=jnp.float32).astype(jnp.int32)

    hit = jnp.any(routes_all == mine, axis=1)
    rank = ranks(hit)
    slots = jnp.arange(capacity, dtype=jnp.int32)
    pick = (hit[:, None, :] & (rank[:, None, :] == slots[None, :, None])).astype(jnp.bfloat16)
    rows = lax.dot_general(
        pick, tok_all, (((2,), (1,)), ((0,), (0,))), preferred_element_type=jnp.float32
    ).astype(jnp.bfloat16)
    rows = rows.reshape(groups * capacity, width)
    gate_pre = jnp.dot(rows, gate_up[0], preferred_element_type=jnp.float32)
    up_pre = jnp.dot(rows, gate_up[1], preferred_element_type=jnp.float32)
    hidden = (jax.nn.silu(gate_pre) * up_pre).astype(jnp.bfloat16)
    results = jnp.dot(hidden, down, preferred_element_type=jnp.float32).astype(jnp.bfloat16)
    returned = lax.all_to_all(
        results.reshape(groups, capacity, width), "expert", split_axis=0, concat_axis=0, tiled=True
    )
    named = routes_t[None, :, :] == jnp.arange(groups, dtype=jnp.int32)[:, None, None]
    out_hit = jnp.any(named, axis=1)
    out_rank = ranks(out_hit)
    weight = jnp.sum(jnp.where(named, route_weight.T[None], 0.0), axis=1)
    place = out_hit[:, None, :] & (out_rank[:, None, :] == slots[None, :, None])
    spread = jnp.where(place, weight[:, None, :], 0.0).reshape(groups * capacity, tok_rows)
    high = spread.astype(jnp.bfloat16)
    low = (spread - high.astype(jnp.float32)).astype(jnp.bfloat16)
    back = returned.reshape(groups * capacity, width)
    mixed = lax.dot_general(
        high, back, (((0,), (0,)), ((), ())), preferred_element_type=jnp.float32
    ) + lax.dot_general(low, back, (((0,), (0,)), ((), ())), preferred_element_type=jnp.float32)
    return mixed.astype(jnp.bfloat16)


def solution(mesh):
    placed = (
        P(("dp", "expert"), None),
        P(("dp", "expert"), None),
        P(("dp", "expert"), None),
        P("expert", None, "dp", None),
        P("expert", None, "dp", None),
        P("expert", None, "dp", None),
        P("expert", None, "dp", None),
        P("expert", "dp", None),
        P("expert", "dp", None),
        P("expert", "dp", None),
        P("expert", "dp", None),
    )
    return jax.shard_map(
        per_device, mesh=mesh, in_specs=placed, out_specs=P(("dp", "expert"), None), check_vma=False
    )
```

time: 472 us -> 373 us (0.79)
  waiting for transfers between devices: 378 us -> 79.7 us
  Pallas kernels: 0 us -> 145 us
  blocking collectives: 0 us -> 37.3 us
  starting transfers between devices: 15.4 us -> 51.8 us
  other arithmetic: 15 us -> 0.08 us
  between operations: 13.6 us -> 0.1 us
  matrix products: 29.8 us -> 36.8 us
    all_to_all x2 -> x1, waiting for transfers between devices: 275 us -> 79.7 us  [per_device(): lax.all_to_all(results.reshape(groups, capacity, width), 'expert', split_...]
    pallas_call x0 -> x1, Pallas kernels: none -> 145 us  [gather_all(): pl.pallas_call(gather_kernel, out_shape=(jax.ShapeDtypeStruct((2, dps, ro...]
    all_gather x2 -> x0, waiting for transfers between devices: 104 us -> none  [the longest x1 104 us: per_device(): lax.all_gather(down_own, 'dp', axis=1, tiled=True)]
    all_gather x0 -> x1, blocking collectives: none -> 37.3 us  [per_device(): routes_all = lax.all_gather(routes_t, 'expert', axis=0)]
    all_to_all x2 -> x1, starting transfers between devices: 15.2 us -> 51.8 us  [per_device(): lax.all_to_all(results.reshape(groups, capacity, width), 'expert', split_...]
    unnamed x14 -> x28, local copies, waits for them, and re-layouts: 0.29 us -> 14.2 us
    gather x3 -> x0, local copies, waits for them, and re-layouts: 13.8 us -> none  [the longest x2 7.95 us: per_device(): jnp.take(back_rows, slot_ids, axis=0).reshape(tok_rows, top_count, width)]
    convert_element_type x3 -> x0, other arithmetic: 9.34 us -> none  [the longest x2 9.34 us: adamw(): (master - learn_rate * (update + weight_decay * master)).astype(jnp.bfloa...]
  transfers between devices with their start and end apart: 4 -> 1, of which waited for: 3 -> 1; matrix products, arithmetic and copies ran while one was open for 6% -> 0% of each run, Pallas kernels for 0% -> 0%
where the time goes in v1:
time: 373 us; the launch traced here: 369 us
  Pallas kernels  145 us (39%)
  waiting for transfers between devices  79.7 us (21%)
  starting transfers between devices  51.8 us (14%)
  blocking collectives  37.3 us (10%)
  matrix products  36.8 us (10%)
  local copies, waits for them, and re-layouts  18.4 us (5%)
    pallas_call x1, Pallas kernels, gather_all(): pl.pallas_call(gather_kernel, out_shape=(jax.ShapeDtypeStruct((2, dps, ro...  145 us
    all_to_all x1, waiting for transfers between devices, per_device(): lax.all_to_all(results.reshape(groups, capacity, width), 'expert', split_...  79.7 us
    all_to_all x1, starting transfers between devices, per_device(): lax.all_to_all(results.reshape(groups, capacity, width), 'expert', split_...  51.8 us
    all_gather x1, blocking collectives, per_device(): routes_all = lax.all_gather(routes_t, 'expert', axis=0)  37.3 us
    dot_general x1, matrix products, per_device(): jnp.dot(hidden, down, preferred_element_type=jnp.float32)  16.3 us
    unnamed x28, local copies, waits for them, and re-layouts  14.2 us
  transfers between devices with their start and end apart: 1, of which 1 were waited for; matrix products, arithmetic and copies ran while one was open for 0% of the time, Pallas kernels for 0%

profile of v1, /device:TPU:32, one launch (start us, length us, event | category | flops | bytes accessed | tf_op | source)
XLA Modules:
  0.0 368.9 jit_solution(8729100729696968708)
XLA Ops:
  0.0 37.3 %all-gather.1 = s32[32,4,128]{2,1,0:T(4,128)S(1)} all-gather(s32[1,4,128]{2,1,0:T(4,128)} %bitcast.49), channel_id=2, replica_groups=mesh['dp'=8,'expert'=32] {'expert'}, dimensions={0}, use_global_device_ids=true | all-gather | bytes 67584 | tf_op jit(solution)/shard_map/all_gather | solution.py:269
  37.3 0.1 compare_reduce_fusion
  37.4 0.1 convolution_convert_fusion.2
  37.5 1.6 copy-done
  39.2 1.6 copy-done.1
  40.8 1.6 copy-done.2
  42.5 1.3 copy-done.3
  43.7 1.3 copy-done.4
  45.0 1.3 copy-done.5
  46.3 1.3 copy-done.6
  47.5 1.1 copy-done.7
  48.6 1.0 copy-done.8
  49.6 144.8 %update_and_gather.1 = (bf16[2,8,224,1280]{3,2,1,0:T(8,128)(2,1)S(1)}, bf16[8,160,1792]{2,1,0:T(8,128)(2,1)S(1)}, bf16[32,128,1792]{2,1,0:T(8,128)(2,1)}) custom-call(bf16[128,1792]{1,0:T(8,128)(2,1)S(1)} %copy-done.8, f32[448,1280]{1,0:T(8,128)S(1)} %bitcast.35, f32[448,1280]{1,0:T(8,128)S(1)} %bitcast.36, f32[448,1280]{1,0:T(8,128)S(1)} %bitcast.37, ...), custom_call_target="tpu_custom_call" | custom-call | tf_op jit(solution)/shard_map/update_and_gather/pallas_call | solution.py:227
  194.4 0.0 copy-start.9
  194.4 2.1 copy-done.9
  196.5 4.2 %fusion.21 = (bf16[1,8,224,1280]{3,2,1,0:T(8,128)(2,1)}, bf16[1,8,224,1280]{3,2,1,0:T(8,128)(2,1)}) fusion(bf16[2,8,224,1280]{3,2,1,0:T(8,128)(2,1)S(1)} %get-tuple-element.9), kind=kLoop, calls=%fused_computation.34 | loop fusion | bytes 18350080 | tf_op jit(solution)/shard_map/slice | solution.py:286
  200.7 7.3 %convolution_convert_fusion.1 = bf16[32,32,1792]{2,1,0:T(8,128)(2,1)S(1)} fusion(bf16[32,128,1792]{2,1,0:T(8,128)(2,1)} %get-tuple-element.8, s32[32,128]{1,0:T(8,128)S(1)} %convolution_convert_fusion.2, pred[32,128]{1,0:T(8,128)(4,1)S(1)} %compare_reduce_fusion), kind=kOutput, calls=%fused_computation.2 | convolution fusion | flops 471859200 | bytes 18370560 | tf_op jit(solution)/shard_map/dot_general | solution.py:281
  208.1 6.6 %fusion.22 = f32[1024,1280]{1,0:T(8,128)} fusion(bf16[1024,1792]{1,0:T(8,128)(2,1)S(1)} %bitcast.44, bf16[1792,1280]{1,0:T(8,128)(2,1)S(1)} %bitcast.47), kind=kOutput, calls=%fused_computation.35 | convolution fusion | flops 4697620480 | bytes 13500416 | tf_op jit(solution)/shard_map/dot_general | solution.py:285
  214.7 16.3 %convolution_convert_fusion = bf16[1024,1792]{1,0:T(8,128)(2,1)} fusion(bf16[1280,1792]{1,0:T(8,128)(2,1)} %bitcast.43, f32[1024,1280]{1,0:T(8,128)} %fusion.22, bf16[1024,1792]{1,0:T(8,128)(2,1)} %bitcast.45, bf16[1792,1280]{1,0:T(8,128)(2,1)} %bitcast.46), kind=kOutput, calls=%fused_computation.1 | convolution fusion | flops 9404940288 | bytes 21757952 | tf_op jit(solution)/shard_map/dot_general | solution.py:288
  231.0 51.8 %all-to-all-start = ((bf16[32,32,1792]{2,1,0:T(8,128)(2,1)}), bf16[32,32,1792]{2,1,0:T(8,128)(2,1)}, u32[]{:S(2)}, u32[]{:S(2)}) async-start(bf16[32,32,1792]{2,1,0:T(8,128)(2,1)} %bitcast.48), calls=%async_computation | async-start | bytes 7340032 | tf_op jit(solution)/shard_map/all_to_all | solution.py:289
  282.8 0.1 convolution_convert_fusion.3
  283.0 79.7 %all-to-all-done = bf16[32,32,1792]{2,1,0:T(8,128)(2,1)} async-done(((bf16[32,32,1792]{2,1,0:T(8,128)(2,1)}), bf16[32,32,1792]{2,1,0:T(8,128)(2,1)}, u32[]{:S(2)}, u32[]{:S(2)}) %all-to-all-start) | async-done | bytes 3670048 | tf_op jit(solution)/shard_map/all_to_all | solution.py:289
  362.7 2.7 convolution_bitcast_fusion
  365.4 3.5 fusion.1
  (19 shorter events, 0.1 us)
Async XLA Ops:
  37.5 1.7 copy-start
  39.2 1.6 copy-start.1
  40.8 1.6 copy-start.2
  42.5 1.3 copy-start.3
  43.7 1.3 copy-start.4
  45.0 1.3 copy-start.5
  46.3 1.3 copy-start.6
  47.5 1.1 copy-start.7
  48.6 1.0 copy-start.8
  194.4 2.1 copy-start.9
  200.7 7.4 %copy-start.11 = (bf16[1,8,224,1280]{3,2,1,0:T(8,128)(2,1)S(1)}, bf16[1,8,224,1280]{3,2,1,0:T(8,128)(2,1)}, u32[]{:S(2)}) copy-start(bf16[1,8,224,1280]{3,2,1,0:T(8,128)(2,1)} %get-tuple-element.12) | copy-start | bytes 13762564
  208.1 6.6 %copy-start.10 = (bf16[32,32,1792]{2,1,0:T(8,128)(2,1)}, bf16[32,32,1792]{2,1,0:T(8,128)(2,1)S(1)}, u32[]{:S(2)}) copy-start(bf16[32,32,1792]{2,1,0:T(8,128)(2,1)S(1)} %convolution_convert_fusion.1) | copy-start | bytes 11010052
  231.0 51.8 %copy-start.12 = (s32[128,4]{0,1:T(4,128)S(1)}, s32[128,4]{0,1:T(4,128)}, u32[]{:S(2)}) copy-start(s32[128,4]{0,1:T(4,128)} %param.12) | copy-start | bytes 6148
  231.0 51.8 %copy-start.13 = (f32[128,4]{0,1:T(4,128)S(1)}, f32[128,4]{0,1:T(4,128)}, u32[]{:S(2)}) copy-start(f32[128,4]{0,1:T(4,128)} %param.13) | copy-start | bytes 6148
  231.0 131.7 %all-to-all-start = ((bf16[32,32,1792]{2,1,0:T(8,128)(2,1)}), bf16[32,32,1792]{2,1,0:T(8,128)(2,1)}, u32[]{:S(2)}, u32[]{:S(2)}) async-start(bf16[32,32,1792]{2,1,0:T(8,128)(2,1)} %bitcast.48), calls=%async_computation | async-start | bytes 7340032 | tf_op jit(solution)/shard_map/all_to_all | solution.py:289

commit v2 on v1

--- a/solution.py
+++ b/solution.py
@@ -57,11 +57,10 @@
         for cp in loads[h]:
             cp.start()
 
-    partners = [{"dp": right, "expert": e}, {"dp": left, "expert": e}, {"dp": mirror, "expert": e}]
-    partners += [{"dp": d, "expert": at_ex(z + k, y, c)} for k in range(1, ZN)]
+    barrier = pltpu.get_barrier_semaphore()
+    partners = [{"dp": p, "expert": e} for p in (right, left, mirror)]
     partners += [{"dp": d, "expert": at_ex(z, y + k, c)} for k in range(1, YN)]
-    partners += [{"dp": d, "expert": at_ex(z, y, 1 - c)}]
-    barrier = pltpu.get_barrier_semaphore()
+    partners += [{"dp": d, "expert": p} for p in (at_ex(z, y, 1 - c), at_ex(z + 1, y, c), at_ex(z - 1, y, c))]
     for p in partners:
         pl.semaphore_signal(barrier, inc=1, device_id=p, device_id_type=MESH)
     pl.semaphore_wait(barrier, len(partners))
@@ -75,37 +74,90 @@
             device_id={"dp": d, "expert": target}, device_id_type=MESH,
         )
 
-    TZ = lambda k: k - 1
-    TY = lambda j, k: 3 + j * 3 + k - 1
-    TS = lambda j, k: 15 + j * 4 + k
-
-    def tok_send(slot, target, op, src=None):
-        cp = tok_copy(slot, target, op, src)
-        cp.start()
-        sent.append(cp)
-
-    def tok_wait(slot, op):
-        tok_copy(slot, at_ex(z, y, 1 - c), op).wait_recv()
+    UP = lambda n: n - 1
+    DOWN = lambda n: 2 + n
+    TY = lambda b, k: 6 + b * 3 + k - 1
+    TS = lambda b, k: 18 + b * 4 + k
+    sibling = at_ex(z, y, 1 - c)
+
+    def tok_spread(b, src=None):
+        slot = at_ex(b, y, c)
+        for k in (1, 3, 2):
+            tok_copy(slot, at_ex(z, y + k, c), TY(b, k), src).start()
+        tok_copy(slot, sibling, TS(b, 0), src).start()
 
     own_tok = pltpu.make_async_copy(tok, tok_all.at[e], keep_sem.at[0])
     own_tok.start()
-    for k in (1, 3, 2):
-        tok_send(e, at_ex(z + k, y, c), TZ(k), tok)
-    for k in (1, 3, 2):
-        tok_send(e, at_ex(z, y + k, c), TY(0, k), tok)
-    tok_send(e, at_ex(z, y, 1 - c), TS(0, 0), tok)
-
-    def tok_z(j):
-        slot = at_ex(z - j, y, c)
-        tok_wait(slot, TZ(j))
-        for k in (1, 3, 2):
-            tok_send(slot, at_ex(z, y + k, c), TY(j, k))
-        tok_send(slot, at_ex(z, y, 1 - c), TS(j, 0))
-
-    def tok_y(j, k):
-        slot = at_ex(z - j, y - k, c)
-        tok_wait(slot, TY(j, k))
-        tok_send(slot, at_ex(z, y, 1 - c), TS(j, k))
+    can_up, can_down = z < ZN - 1, z > 0
+
+    @pl.when(can_up)
+    def _():
+        tok_copy(e, at_ex(z + 1, y, c), UP(1), tok).start()
+
+    @pl.when(can_down)
+    def _():
+        tok_copy(e, at_ex(z - 1, y, c), DOWN(1), tok).start()
+
+    tok_spread(z, tok)
+
+    def tok_z(n):
+        @pl.when(z >= n)
+        def _():
+            slot = at_ex(z - n, y, c)
+            tok_copy(slot, sibling, UP(n)).wait_recv()
+
+            if n < ZN - 1:
+
+                @pl.when(can_up)
+                def _():
+                    tok_copy(slot, at_ex(z + 1, y, c), UP(n + 1)).start()
+
+            tok_spread(z - n)
+
+        @pl.when(z < ZN - n)
+        def _():
+            slot = at_ex(z + n, y, c)
+            tok_copy(slot, sibling, DOWN(n)).wait_recv()
+
+            if n < ZN - 1:
+
+                @pl.when(can_down)
+                def _():
+                    tok_copy(slot, at_ex(z - 1, y, c), DOWN(n + 1)).start()
+
+            tok_spread(z + n)
+
+    def tok_y(n):
+        def hand_on(b):
+            for k in (1, 3, 2):
+                slot = at_ex(b, y - k, c)
+                tok_copy(slot, sibling, TY(b, k)).wait_recv()
+                tok_copy(slot, sibling, TS(b, k)).start()
+
+        if n == 0:
+            hand_on(z)
+            return
+        pl.when(z >= n)(lambda: hand_on(z - n))
+        pl.when(z < ZN - n)(lambda: hand_on(z + n))
+
+    def tok_finish():
+        for b in range(ZN):
+            for k in range(YN):
+                tok_copy(at_ex(b, y - k, 1 - c), sibling, TS(b, k)).wait_recv()
+        for b in range(ZN):
+            for k in range(1, YN):
+                tok_copy(e, sibling, TY(b, k)).wait_send()
+            for k in range(YN):
+                tok_copy(e, sibling, TS(b, k)).wait_send()
+        for n in range(1, ZN):
+
+            @pl.when(jnp.logical_and(can_up, z >= n - 1))
+            def _():
+                tok_copy(e, sibling, UP(n)).wait_send()
+
+            @pl.when(jnp.logical_and(can_down, z <= ZN - n))
+            def _():
+                tok_copy(e, sibling, DOWN(n)).wait_send()
 
     def slot_of(h, owner):
         if h < 4:
@@ -149,7 +201,8 @@
             return 0
 
         lax.fori_loop(0, rows // 16, step, 0)
-        w_send_to(h, d, mirror, MIR, own_of(h))
+        if h < 2:
+            w_copy(h, d, mirror, MIR, own_of(h)).start()
         w_send_to(h, d, right, R_OWN, own_of(h))
         w_send_to(h, d, left, L_OWN, own_of(h))
         keep = pltpu.make_async_copy(own_of(h), slot_of(h, d), keep_sem.at[1 + h])
@@ -164,6 +217,10 @@
         else:
             w_send_to(h, right, left, F_OWN)
 
+    def to_mirror(h):
+        w_copy(h - 2, d, mirror, MIR, own_of(h - 2)).wait_send()
+        w_copy(h, d, mirror, MIR, own_of(h)).start()
+
     def from_mirror(h):
         w_wait(h, mirror, MIR)
         w_send_to(h, mirror, right, R_P)
@@ -177,41 +234,41 @@
         else:
             w_send_to(h, p_right, left, F_P)
 
+    tok_z(1)
     fwd_own(0)
-    tok_z(1)
     fwd_own(1)
+    to_mirror(2)
+    tok_z(2)
+    fwd_own(2)
+    fwd_own(3)
+    to_mirror(3)
     tok_z(3)
+    fwd_own(4)
+    fwd_own(5)
     from_mirror(0)
-    fwd_own(2)
-    tok_z(2)
-    fwd_own(3)
+    to_mirror(4)
+    tok_y(0)
     from_mirror(1)
-    fwd_own(4)
+    fwd_mirror(0)
+    to_mirror(5)
+    tok_y(1)
     from_mirror(2)
-    fwd_own(5)
-    for k in (1, 3, 2):
-        tok_y(0, k)
-    fwd_mirror(0)
+    fwd_mirror(1)
+    tok_y(2)
     from_mirror(3)
-    fwd_mirror(1)
-    for k in (1, 3, 2):
-        tok_y(1, k)
+    fwd_mirror(2)
+    tok_y(3)
     from_mirror(4)
-    fwd_mirror(2)
-    for k in (1, 3, 2):
-        tok_y(3, k)
+    fwd_mirror(3)
     from_mirror(5)
-    fwd_mirror(3)
-    for k in (1, 3, 2):
-        tok_y(2, k)
     fwd_mirror(4)
     fwd_mirror(5)
     for h in range(HALVES):
         w_wait(h, far, F_OWN)
         w_wait(h, p_far, F_P)
-    for j in range(ZN):
-        for k in range(YN):
-            tok_wait(at_ex(z - j, y - k, 1 - c), TS(j, k))
+    for h in (4, 5):
+        w_copy(h, d, mirror, MIR, own_of(h)).wait_send()
+    tok_finish()
     for cp in keeps:
         cp.wait()
     for cp in sent:
@@ -241,12 +298,12 @@
             pltpu.SemaphoreType.DMA((HALVES + 1,)),
             pltpu.SemaphoreType.DMA((7 * HALVES,)),
             pltpu.SemaphoreType.DMA((7 * HALVES,)),
-            pltpu.SemaphoreType.DMA((31,)),
-            pltpu.SemaphoreType.DMA((31,)),
+            pltpu.SemaphoreType.DMA((34,)),
+            pltpu.SemaphoreType.DMA((34,)),
         ],
         name="update_and_gather",
         compiler_params=pltpu.CompilerParams(
-            collective_id=0, has_side_effects=True, vmem_limit_bytes=24 * 2**20
+            collective_id=0, has_side_effects=True, vmem_limit_bytes=60 * 2**20
         ),
     )(tokens, w_in, m_in, v_in, g_in, w_out, m_out, v_out, g_out)
 
@@ -258,15 +315,20 @@
     top_count = routes.shape[1]
     capacity = 2 * tok_rows * top_count // groups
     two, depth, wide = w_in.shape[1:]
+    whole = -(-(width + 3 * top_count) // 128) * 128
+    high = lax.reduce_precision(route_weight, 8, 7)
+    low = route_weight - high
+    packed = [tokens] + [a.astype(jnp.bfloat16) for a in (routes, high, low)]
+    packed += [jnp.zeros((tok_rows, whole - width - 3 * top_count), jnp.bfloat16)]
     gu, dn, tok_all = gather_all(
-        tokens,
+        jnp.concatenate(packed, axis=1),
         *(a.reshape(two * depth, wide) for a in (w_in, m_in, v_in, g_in)),
         *(a.reshape(a.shape[1:]) for a in (w_out, m_out, v_out, g_out)),
     )
     gate_up = gu.reshape(two, -1, wide)
     down = dn.reshape(-1, width)
     routes_t = routes.T
-    routes_all = lax.all_gather(routes_t, "expert", axis=0)
+    routes_all = tok_all[:, :, width : width + top_count].astype(jnp.int32)
     upper = (
         jnp.arange(tok_rows)[:, None] < jnp.arange(tok_rows)[None, :]
     ).astype(jnp.bfloat16)
@@ -274,12 +336,12 @@
     def ranks(hit):
         return jnp.dot(hit.astype(jnp.bfloat16), upper, preferred_element_type=jnp.float32).astype(jnp.int32)
 
-    hit = jnp.any(routes_all == mine, axis=1)
+    hit = jnp.any(routes_all == mine, axis=2)
     rank = ranks(hit)
     slots = jnp.arange(capacity, dtype=jnp.int32)
     pick = (hit[:, None, :] & (rank[:, None, :] == slots[None, :, None])).astype(jnp.bfloat16)
     rows = lax.dot_general(
-        pick, tok_all, (((2,), (1,)), ((0,), (0,))), preferred_element_type=jnp.float32
+        pick, tok_all[:, :, :width], (((2,), (1,)), ((0,), (0,))), preferred_element_type=jnp.float32
     ).astype(jnp.bfloat16)
     rows = rows.reshape(groups * capacity, width)
     gate_pre = jnp.dot(rows, gate_up[0], preferred_element_type=jnp.float32)

time: 373 us -> 294 us (0.79)
  blocking collectives: 37.3 us -> 0 us
  starting transfers between devices: 51.8 us -> 19.7 us
  local copies, waits for them, and re-layouts: 18.4 us -> 7.22 us
  Pallas kernels: 145 us -> 137 us
  matrix products: 36.8 us -> 42.7 us
    all_gather x1 -> x0, blocking collectives: 37.3 us -> none  [per_device(): routes_all = lax.all_gather(routes_t, 'expert', axis=0)]
    all_to_all x1, starting transfers between devices: 51.8 us -> 19.7 us  [per_device(): lax.all_to_all(results.reshape(groups, capacity, width), 'expert', split_...]
    unnamed x28 -> x11, local copies, waits for them, and re-layouts: 14.2 us -> 0.81 us
    pallas_call x1, Pallas kernels: 145 us -> 137 us  [gather_all(): pl.pallas_call(gather_kernel, out_shape=(jax.ShapeDtypeStruct((2, dps, ro...]
    dot_general x1, matrix products: 6.59 us -> 10.6 us  [per_device(): gate_pre = jnp.dot(rows, gate_up[0], preferred_element_type=jnp.float32)]
where the time goes in v2:
time: 294 us; the launch traced here: 290 us
  Pallas kernels  137 us (47%)
  waiting for transfers between devices  79.7 us (27%)
  matrix products  42.7 us (15%)
  starting transfers between devices  19.7 us (7%)
  local copies, waits for them, and re-layouts  7.22 us (2%)
  other arithmetic  3.41 us (1%)
    pallas_call x1, Pallas kernels, gather_all(): pl.pallas_call(gather_kernel, out_shape=(jax.ShapeDtypeStruct((2, dps, ro...  137 us
    all_to_all x1, waiting for transfers between devices, per_device(): lax.all_to_all(results.reshape(groups, capacity, width), 'expert', split_...  79.7 us
    all_to_all x1, starting transfers between devices, per_device(): lax.all_to_all(results.reshape(groups, capacity, width), 'expert', split_...  19.7 us
    dot_general x1, matrix products, per_device(): jnp.dot(hidden, down, preferred_element_type=jnp.float32)  16.4 us
    dot_general x1, matrix products, per_device(): gate_pre = jnp.dot(rows, gate_up[0], preferred_element_type=jnp.float32)  10.6 us
    dot_general x1, matrix products, per_device(): lax.dot_general(pick, tok_all[:, :, :width], (((2,), (1,)), ((0,), (0,)))...  9.16 us
  transfers between devices with their start and end apart: 1, of which 1 were waited for; matrix products, arithmetic and copies ran while one was open for 0% of the time, Pallas kernels for 0%

profile of v2, /device:TPU:32, one launch (start us, length us, event | category | flops | bytes accessed | tf_op | source)
XLA Modules:
  0.0 290.2 jit_solution(2450247512938981284)
XLA Ops:
  0.0 0.7 fusion.28
  0.7 0.8 copy.18
  1.5 0.1 copy.19
  1.6 0.1 copy.21
  1.7 0.7 convert_element_type.49
  2.4 0.1 copy.20
  2.6 1.9 concatenate.3.tok
  4.4 137.4 %update_and_gather.1 = (bf16[2,8,224,1280]{3,2,1,0:T(8,128)(2,1)}, bf16[8,160,1792]{2,1,0:T(8,128)(2,1)}, bf16[32,128,1920]{2,1,0:T(8,128)(2,1)}) custom-call(bf16[128,1920]{1,0:T(8,128)(2,1)} %concatenate.3.tok, f32[448,1280]{1,0:T(8,128)} %bitcast.39, f32[448,1280]{1,0:T(8,128)} %bitcast.40, f32[448,1280]{1,0:T(8,128)} %bitcast.41, ...), custom_call_target="tpu_custom_call" | custom-call | tf_op jit(solution)/shard_map/update_and_gather/pallas_call | solution.py:284
  141.9 0.0 slice-start
  141.9 2.0 fusion.7
  143.9 0.1 convolution_convert_fusion.1
  144.0 9.2 %fusion.2 = bf16[32,32,1792]{2,1,0:T(8,128)(2,1)} fusion(bf16[32,128,1920]{2,1,0:T(8,128)(2,1)} %get-tuple-element.8, s32[32,128]{1,0:T(8,128)S(1)} %convolution_convert_fusion.1, pred[32,128]{1,0:T(8,128)(4,1)S(1)} %fusion.7), kind=kOutput, calls=%fused_computation.3 | convolution fusion | flops 471859200 | bytes 18370560 | tf_op jit(solution)/shard_map/dot_general | solution.py:343
  153.2 0.0 slice-done
  153.2 0.0 slice-done.1
  153.2 0.0 slice-done.2
  153.2 4.2 %fusion.27 = (bf16[1,8,224,1280]{3,2,1,0:T(8,128)(2,1)}, bf16[1,8,224,1280]{3,2,1,0:T(8,128)(2,1)}) fusion(bf16[2,8,224,1280]{3,2,1,0:T(8,128)(2,1)S(1)} %bitcast.33), kind=kLoop, calls=%fused_computation.39 | loop fusion | bytes 18350080 | tf_op jit(solution)/shard_map/slice | solution.py:348
  157.4 10.6 %fusion.29 = f32[1024,1280]{1,0:T(8,128)} fusion(bf16[1024,1792]{1,0:T(8,128)(2,1)} %bitcast.37, bf16[1792,1280]{1,0:T(8,128)(2,1)} %bitcast.35), kind=kOutput, calls=%fused_computation.41 | convolution fusion | flops 4697620480 | bytes 13500416 | tf_op jit(solution)/shard_map/dot_general | solution.py:347
  168.0 16.4 %convolution_convert_fusion = bf16[1024,1792]{1,0:T(8,128)(2,1)} fusion(bf16[1280,1792]{1,0:T(8,128)(2,1)} %bitcast.50, f32[1024,1280]{1,0:T(8,128)} %fusion.29, bf16[1024,1792]{1,0:T(8,128)(2,1)} %bitcast.38, bf16[1792,1280]{1,0:T(8,128)(2,1)} %bitcast.34), kind=kOutput, calls=%fused_computation.4 | convolution fusion | flops 9404940288 | bytes 21757952 | tf_op jit(solution)/shard_map/dot_general | solution.py:350
  184.4 19.7 %all-to-all-start = ((bf16[32,32,1792]{2,1,0:T(8,128)(2,1)}), bf16[32,32,1792]{2,1,0:T(8,128)(2,1)}, u32[]{:S(2)}, u32[]{:S(2)}) async-start(bf16[32,32,1792]{2,1,0:T(8,128)(2,1)} %bitcast.36), calls=%async_computation | async-start | bytes 7340032 | tf_op jit(solution)/shard_map/all_to_all | solution.py:351
  204.1 0.0 copy-done
  204.1 0.1 convolution_convert_fusion.2
  204.3 79.7 %all-to-all-done = bf16[32,32,1792]{2,1,0:T(8,128)(2,1)} async-done(((bf16[32,32,1792]{2,1,0:T(8,128)(2,1)}), bf16[32,32,1792]{2,1,0:T(8,128)(2,1)}, u32[]{:S(2)}, u32[]{:S(2)}) %all-to-all-start) | async-done | bytes 3670048 | tf_op jit(solution)/shard_map/all_to_all | solution.py:351
  283.9 2.7 convolution_bitcast_fusion
  286.7 3.5 %fusion.6 = bf16[128,1792]{1,0:T(8,128)(2,1)} fusion(f32[128,1792]{1,0:T(8,128)S(1)} %convolution_bitcast_fusion, bf16[32,32,1792]{2,1,0:T(8,128)(2,1)} %all-to-all-done, f32[32,128]{1,0:T(8,128)S(1)} %select_reduce_fusion, s32[32,128]{1,0:T(8,128)S(1)} %convolution_convert_fusion.2, pred[32,128]{1,0:T(8,128)(4,1)S(1)} %fusion.23), kind=kOutput, calls=%fused_computation.8 | convolution fusion | flops 470614016 | bytes 5083136 | tf_op jit(solution)/shard_map/dot_general | solution.py:363
  (10 shorter events, 0.1 us)
Async XLA Ops:
  141.9 11.3 %slice-start = ((s8[9175040]{0:T(1024)(128)(4,1)}), s8[4194304]{0:T(1024)(128)(4,1)S(1)}, s32[]{:S(2)}) async-start(s8[9175040]{0:T(1024)(128)(4,1)} %bitcast.32), calls=%async_computation.1 | async-start | bytes 8388608
  144.0 9.2 %slice-start.1 = ((s8[9175040]{0:T(1024)(128)(4,1)}), s8[4194304]{0:T(1024)(128)(4,1)S(1)}, s32[]{:S(2)}) async-start(s8[9175040]{0:T(1024)(128)(4,1)} %bitcast.32), calls=%async_computation.2 | async-start | bytes 8388608
  144.0 9.2 %slice-start.2 = ((s8[9175040]{0:T(1024)(128)(4,1)}), s8[786432]{0:T(1024)(128)(4,1)S(1)}, s32[]{:S(2)}) async-start(s8[9175040]{0:T(1024)(128)(4,1)} %bitcast.32), calls=%async_computation.3 | async-start | bytes 1572864
  184.4 19.7 %copy-start = (s32[128,4]{0,1:T(4,128)S(1)}, s32[128,4]{0,1:T(4,128)}, u32[]{:S(2)}) copy-start(s32[128,4]{0,1:T(4,128)} %param.12) | copy-start | bytes 6148
  184.4 19.7 %copy-start.1 = (f32[128,4]{0,1:T(4,128)S(1)}, f32[128,4]{0,1:T(4,128)}, u32[]{:S(2)}) copy-start(f32[128,4]{0,1:T(4,128)} %param.13) | copy-start | bytes 6148
  184.4 99.5 %all-to-all-start = ((bf16[32,32,1792]{2,1,0:T(8,128)(2,1)}), bf16[32,32,1792]{2,1,0:T(8,128)(2,1)}, u32[]{:S(2)}, u32[]{:S(2)}) async-start(bf16[32,32,1792]{2,1,0:T(8,128)(2,1)} %bitcast.36), calls=%async_computation | async-start | bytes 7340032 | tf_op jit(solution)/shard_map/all_to_all | solution.py:351

commit v3 on v2

v3 whole, which is shorter than its diff:
```python
import jax
import jax.numpy as jnp
from jax import lax
from jax.experimental import pallas as pl
from jax.experimental.pallas import tpu as pltpu
from jax.sharding import PartitionSpec as P

MESH = pl.DeviceIdType.MESH
beta_one = 0.9
beta_two = 0.95
corr_one = 0.99997343860111
corr_two = 0.99407947077967
adam_eps = 1e-08
learn_rate = 0.01
weight_decay = 0.1
XN, YN, ZN = 4, 4, 4
TOPW = 4
HALVES = 6


def adamw(master, moment, second, gradient):
    grad_value = gradient.astype(jnp.float32)
    moment_new = beta_one * moment + (1.0 - beta_one) * grad_value
    second_new = beta_two * second + (1.0 - beta_two) * grad_value * grad_value
    update = moment_new / corr_one / (jnp.sqrt(second_new / corr_two) + adam_eps)
    return (master - learn_rate * (update + weight_decay * master)).astype(jnp.bfloat16)


def layer_kernel(
    tok, w_in, m_in, v_in, g_in, w_out, m_out, v_out, g_out,
    mixed, tok_all,
    wi, mi, vi, gi, wo, mo, vo, go, gu_v, dn_v,
    tbuf, meta, rows_v, gate_v, hid_v, res_v, ry_v, part_v, sib_v, sum_v, zin_v,
    load_sem, keep_sem, w_send, w_recv, t_send, t_recv, tin_sem, y_send, y_recv, s_send, s_recv, z_send, z_recv,
):
    d, e = lax.axis_index("dp"), lax.axis_index("expert")
    zh, x = d // XN, d % XN
    z, y, c = e // (2 * YN), e // 2 % YN, e % 2
    at_dp = lambda h, i: h * XN + lax.rem(i + XN, XN)
    right, left, far = at_dp(zh, x + 1), at_dp(zh, x - 1), at_dp(zh, x + 2)
    mirror = at_dp(1 - zh, x)
    p_right, p_left, p_far = at_dp(1 - zh, x + 1), at_dp(1 - zh, x - 1), at_dp(1 - zh, x + 2)
    at_ex = lambda zz, yy, cc: lax.rem(zz + ZN, ZN) * (2 * YN) + lax.rem(yy + YN, YN) * 2 + cc

    half_in, half_out = w_in.shape[0] // 4, w_out.shape[0] // 2
    loads = []
    for h in range(HALVES):
        pairs = (
            ((w_in, wi), (m_in, mi), (v_in, vi), (g_in, gi))
            if h < 4
            else ((w_out, wo), (m_out, mo), (v_out, vo), (g_out, go))
        )
        rows = pl.ds(h * half_in, half_in) if h < 4 else pl.ds((h - 4) * half_out, half_out)
        loads.append(
            [pltpu.make_async_copy(a.at[rows], b.at[rows], load_sem.at[h, i]) for i, (a, b) in enumerate(pairs)]
        )
        for cp in loads[h]:
            cp.start()

    barrier = pltpu.get_barrier_semaphore()
    partners = [{"dp": p, "expert": e} for p in (right, left, mirror)]
    partners += [{"dp": d, "expert": at_ex(z, y + k, c)} for k in range(1, YN)]
    partners += [{"dp": d, "expert": at_ex(z + k, y, c)} for k in range(1, ZN)]
    partners += [{"dp": d, "expert": at_ex(z, y, 1 - c)}]
    for p in partners:
        pl.semaphore_signal(barrier, inc=1, device_id=p, device_id_type=MESH)
    pl.semaphore_wait(barrier, len(partners))

    sent = []

    def tok_copy(slot, target, op, src=None):
        return pltpu.make_async_remote_copy(
            src_ref=tok_all.at[slot] if src is None else src, dst_ref=tok_all.at[slot],
            send_sem=t_send.at[op], recv_sem=t_recv.at[op],
            device_id={"dp": d, "expert": target}, device_id_type=MESH,
        )

    UP = lambda n: n - 1
    DOWN = lambda n: 2 + n
    TY = lambda b, k: 6 + b * 3 + k - 1
    TS = lambda b, k: 18 + b * 4 + k
    sibling = at_ex(z, y, 1 - c)

    def tok_spread(b, src=None):
        slot = at_ex(b, y, c)
        for k in (1, 3, 2):
            tok_copy(slot, at_ex(z, y + k, c), TY(b, k), src).start()
        tok_copy(slot, sibling, TS(b, 0), src).start()

    own_tok = pltpu.make_async_copy(tok, tok_all.at[e], keep_sem.at[0])
    own_tok.start()
    can_up, can_down = z < ZN - 1, z > 0

    @pl.when(can_up)
    def _():
        tok_copy(e, at_ex(z + 1, y, c), UP(1), tok).start()

    @pl.when(can_down)
    def _():
        tok_copy(e, at_ex(z - 1, y, c), DOWN(1), tok).start()

    tok_spread(z, tok)

    def tok_z(n):
        @pl.when(z >= n)
        def _():
            slot = at_ex(z - n, y, c)
            tok_copy(slot, sibling, UP(n)).wait_recv()

            if n < ZN - 1:

                @pl.when(can_up)
                def _():
                    tok_copy(slot, at_ex(z + 1, y, c), UP(n + 1)).start()

            tok_spread(z - n)

        @pl.when(z < ZN - n)
        def _():
            slot = at_ex(z + n, y, c)
            tok_copy(slot, sibling, DOWN(n)).wait_recv()

            if n < ZN - 1:

                @pl.when(can_down)
                def _():
                    tok_copy(slot, at_ex(z - 1, y, c), DOWN(n + 1)).start()

            tok_spread(z + n)

    def tok_y(n):
        def hand_on(b):
            for k in (1, 3, 2):
                slot = at_ex(b, y - k, c)
                tok_copy(slot, sibling, TY(b, k)).wait_recv()
                tok_copy(slot, sibling, TS(b, k)).start()

        if n == 0:
            hand_on(z)
            return
        pl.when(z >= n)(lambda: hand_on(z - n))
        pl.when(z < ZN - n)(lambda: hand_on(z + n))

    def tok_arrive():
        for b in range(ZN):
            for k in range(YN):
                tok_copy(at_ex(b, y - k, 1 - c), sibling, TS(b, k)).wait_recv()

    def tok_finish():
        for b in range(ZN):
            for k in range(1, YN):
                tok_copy(e, sibling, TY(b, k)).wait_send()
            for k in range(YN):
                tok_copy(e, sibling, TS(b, k)).wait_send()
        for n in range(1, ZN):

            @pl.when(jnp.logical_and(can_up, z >= n - 1))
            def _():
                tok_copy(e, sibling, UP(n)).wait_send()

            @pl.when(jnp.logical_and(can_down, z <= ZN - n))
            def _():
                tok_copy(e, sibling, DOWN(n)).wait_send()

    def slot_of(h, owner):
        if h < 4:
            first = pl.multiple_of(owner * (2 * half_in) + h % 2 * half_in, 16)
            return gu_v.at[h // 2, pl.ds(first, half_in)]
        first = pl.multiple_of(owner * (2 * half_out) + (h - 4) * half_out, 16)
        return dn_v.at[pl.ds(first, half_out)]

    def w_copy(h, owner, target, kind):
        op = kind * HALVES + h
        return pltpu.make_async_remote_copy(
            src_ref=slot_of(h, owner), dst_ref=slot_of(h, owner),
            send_sem=w_send.at[op], recv_sem=w_recv.at[op],
            device_id={"dp": target, "expert": e}, device_id_type=MESH,
        )

    R_OWN, L_OWN, MIR, F_OWN, R_P, L_P, F_P = range(7)

    def w_send_to(h, owner, target, kind):
        cp = w_copy(h, owner, target, kind)
        cp.start()
        sent.append(cp)

    def w_wait(h, owner, kind):
        w_copy(h, owner, right, kind).wait_recv()

    for h in range(HALVES):
        for cp in loads[h]:
            cp.wait()
        a, b, v, g, out, count, first = (
            (wi, mi, vi, gi, gu_v.at[h // 2], half_in, h * half_in)
            if h < 4
            else (wo, mo, vo, go, dn_v, half_out, (h - 4) * half_out)
        )
        base = d * (2 * half_in) + h % 2 * half_in if h < 4 else d * (2 * half_out) + (h - 4) * half_out

        def step(i, _, a=a, b=b, v=v, g=g, out=out, first=first, base=base):
            at = pl.ds(pl.multiple_of(first + i * 16, 16), 16)
            out[pl.ds(pl.multiple_of(base + i * 16, 16), 16), :] = adamw(a[at, :], b[at, :], v[at, :], g[at, :])
            return 0

        lax.fori_loop(0, count // 16, step, 0)
        if h < 2:
            w_copy(h, d, mirror, MIR).start()
        w_send_to(h, d, right, R_OWN)
        w_send_to(h, d, left, L_OWN)

    def fwd_own(h):
        w_wait(h, left, R_OWN)
        w_wait(h, right, L_OWN)
        if h % 2 == 0:
            w_send_to(h, left, right, F_OWN)
        else:
            w_send_to(h, right, left, F_OWN)

    def to_mirror(h):
        w_copy(h - 2, d, mirror, MIR).wait_send()
        w_copy(h, d, mirror, MIR).start()

    def from_mirror(h):
        w_wait(h, mirror, MIR)
        w_send_to(h, mirror, right, R_P)
        w_send_to(h, mirror, left, L_P)

    def fwd_mirror(h):
        w_wait(h, p_left, R_P)
        w_wait(h, p_right, L_P)
        if h % 2 == 0:
            w_send_to(h, p_left, right, F_P)
        else:
            w_send_to(h, p_right, left, F_P)

    width, wide = dn_v.shape[1], dn_v.shape[0]
    tok_rows = tok.shape[0]
    blocks = tok_all.shape[0]
    cap = rows_v.shape[0] // blocks
    f32, bf16 = jnp.float32, jnp.bfloat16

    def iota(shape, dim):
        return lax.broadcasted_iota(jnp.int32, shape, dim)

    def routed(info, expert, slot):
        lanes = expert.shape[1]
        hit = jnp.zeros((tok_rows, lanes), f32)
        weight = jnp.zeros((tok_rows, lanes), f32)
        for k in range(TOPW):
            same = info[:, k : k + 1] == expert
            hit = jnp.where(same, 1.0, hit)
            share = info[:, TOPW + k : TOPW + k + 1] + info[:, 2 * TOPW + k : 2 * TOPW + k + 1]
            weight = jnp.where(same, share, weight)
        earlier = (iota((tok_rows, tok_rows), 1) < iota((tok_rows, tok_rows), 0)).astype(bf16)
        rank = jnp.dot(earlier, hit.astype(bf16), preferred_element_type=f32)
        return jnp.logical_and(rank == slot, hit > 0.0), weight

    def tok_in(s):
        return pltpu.make_async_copy(tok_all.at[s], tbuf.at[lax.rem(s, 2)], tin_sem.at[lax.rem(s, 2)])

    def pick_rows():
        tok_in(0).start()

        def step(s, _):
            @pl.when(s < blocks - 1)
            def _():
                tok_in(s + 1).start()

            tok_in(s).wait()
            at = lax.rem(s, 2)
            info = tbuf[at, :, width:]
            meta[s] = info
            ours = jnp.zeros((1, cap), f32) + e.astype(f32)
            place, _ = routed(info.astype(f32), ours, iota((1, cap), 1).astype(f32))
            picked = lax.dot_general(
                jnp.where(place, 1.0, 0.0).astype(bf16), tbuf[at, :, :width],
                (((0,), (0,)), ((), ())), preferred_element_type=f32,
            )
            rows_v[pl.ds(pl.multiple_of(s * cap, cap), cap), :] = picked.astype(bf16)
            return 0

        lax.fori_loop(0, blocks, step, 0)

    tall, tile = 512, 256

    def up_tiles(gated):
        def step(i, _):
            at = pl.ds(pl.multiple_of(lax.rem(i, 2) * tall, tall), tall)
            cols = pl.ds(pl.multiple_of(i // 2 * tile, tile), tile)
            product = jnp.dot(rows_v[at, :], gu_v[1 if gated else 0, :, cols], preferred_element_type=f32)
            if gated:
                hid_v[at, cols] = (jax.nn.silu(gate_v[at, cols]) * product).astype(bf16)
            else:
                gate_v[at, cols] = product
            return 0

        lax.fori_loop(0, 2 * wide // tile, step, 0)

    group = rows_v.shape[0] // ZN
    pair = 2 * cap

    def y_copy(i, zt, k, to):
        return pltpu.make_async_remote_copy(
            src_ref=res_v.at[zt, pl.ds(pl.multiple_of(to * pair, pair), pair)], dst_ref=ry_v.at[zt, pl.ds(pl.multiple_of(y * pair, pair), pair)],
            send_sem=y_send.at[i, k - 1], recv_sem=y_recv.at[i, k - 1],
            device_id={"dp": d, "expert": at_ex(z, to, c)}, device_id_type=MESH,
        )

    def down(i, zt):
        def step(n, _):
            cols = pl.ds(pl.multiple_of(n * tile, tile), tile)
            mine = pl.ds(pl.multiple_of(zt * group, group), group)
            res_v[zt, :, cols] = jnp.dot(hid_v[mine, :], dn_v[:, cols], preferred_element_type=f32).astype(bf16)
            return 0

        lax.fori_loop(0, width // tile, step, 0)
        for k in (1, 3, 2):
            y_copy(i, zt, k, lax.rem(y + k, YN)).start()
        own = pl.ds(pl.multiple_of(y * pair, pair), pair)
        ry_v[zt, own, :] = res_v[zt, own, :]

    def s_copy(i, zt):
        return pltpu.make_async_remote_copy(
            src_ref=part_v.at[zt, 1 - c], dst_ref=sib_v.at[zt], send_sem=s_send.at[i], recv_sem=s_recv.at[i],
            device_id={"dp": d, "expert": sibling}, device_id_type=MESH,
        )

    def z_copy(j, zt):
        return pltpu.make_async_remote_copy(
            src_ref=sum_v.at[zt], dst_ref=zin_v.at[j - 1], send_sem=z_send.at[j - 1], recv_sem=z_recv.at[j - 1],
            device_id={"dp": d, "expert": at_ex(zt, y, c)}, device_id_type=MESH,
        )

    def partial(i, zt):
        for k in range(1, YN):
            y_copy(i, zt, k, y).wait_recv()
        lane = iota((1, YN * pair), 1)
        expert = (z * (2 * YN) + lane // pair * 2 + c).astype(f32)
        slot = lax.rem(lane, cap).astype(f32)
        spread = []
        for cc in range(2):
            place, weight = routed(meta[zt * (2 * YN) + y * 2 + cc].astype(f32), expert, slot)
            place = jnp.logical_and(place, lax.rem(lane // cap, 2) == cc)
            spread.append(jnp.where(place, weight, 0.0))
        spread = jnp.concatenate(spread, axis=0)
        high = spread.astype(bf16)
        low = (spread - high.astype(f32)).astype(bf16)

        def step(n, _):
            cols = pl.ds(pl.multiple_of(n * tile, tile), tile)
            arrived = ry_v[zt, :, cols]
            total = jnp.dot(high, arrived, preferred_element_type=f32) + jnp.dot(low, arrived, preferred_element_type=f32)
            part_v[zt, 0, :, cols] = total[:tok_rows].astype(bf16)
            part_v[zt, 1, :, cols] = total[tok_rows:].astype(bf16)
            return 0

        lax.fori_loop(0, width // tile, step, 0)
        s_copy(i, zt).start()

    def both_cores(i, zt):
        s_copy(i, zt).wait_recv()

        def step(n, _):
            at = pl.ds(pl.multiple_of(n * 16, 16), 16)
            sum_v[zt, at, :] = (part_v[zt, c, at, :].astype(f32) + sib_v[zt, at, :].astype(f32)).astype(bf16)
            return 0

        lax.fori_loop(0, tok_rows // 16, step, 0)

    tok_z(1)
    fwd_own(0)
    fwd_own(1)
    to_mirror(2)
    tok_z(2)
    fwd_own(2)
    fwd_own(3)
    to_mirror(3)
    tok_z(3)
    fwd_own(4)
    fwd_own(5)
    from_mirror(0)
    to_mirror(4)
    tok_y(0)
    from_mirror(1)
    fwd_mirror(0)
    to_mirror(5)
    tok_y(1)
    from_mirror(2)
    fwd_mirror(1)
    tok_y(2)
    tok_y(3)
    from_mirror(3)
    fwd_mirror(2)
    own_tok.wait()
    tok_arrive()
    pick_rows()
    from_mirror(4)
    fwd_mirror(3)
    for h in (0, 1):
        w_wait(h, far, F_OWN)
        w_wait(h, p_far, F_P)
    up_tiles(False)
    from_mirror(5)
    fwd_mirror(4)
    fwd_mirror(5)
    for h in (2, 3):
        w_wait(h, far, F_OWN)
        w_wait(h, p_far, F_P)
    up_tiles(True)
    for h in (4, 5):
        w_wait(h, far, F_OWN)
        w_wait(h, p_far, F_P)
    order = [(i, j, lax.rem(z + j, ZN)) for i, j in enumerate((2, 1, 3, 0))]
    for i, j, zt in order:
        down(i, zt)
    for i, j, zt in order:
        partial(i, zt)
        both_cores(i, zt)
        if j:
            z_copy(j, zt).start()
    for j in range(1, ZN):
        z_copy(j, z).wait_recv()

    def step(n, _):
        at = pl.ds(pl.multiple_of(n * 16, 16), 16)
        total = sum_v[z, at, :].astype(f32)
        for j in range(ZN - 1):
            total = total + zin_v[j, at, :].astype(f32)
        mixed[at, :] = total.astype(bf16)
        return 0

    lax.fori_loop(0, tok_rows // 16, step, 0)
    for i, j, zt in order:
        for k in range(1, YN):
            y_copy(i, zt, k, lax.rem(y + k, YN)).wait_send()
        s_copy(i, zt).wait_send()
        if j:
            z_copy(j, zt).wait_send()
    for h in (4, 5):
        w_copy(h, d, mirror, MIR).wait_send()
    tok_finish()
    for cp in sent:
        cp.wait_send()


def layer(tokens, w_in, m_in, v_in, g_in, w_out, m_out, v_out, g_out):
    rows_in, wide = w_in.shape
    rows_out, width = w_out.shape
    groups, dps = lax.axis_size("expert"), lax.axis_size("dp")
    tok_rows, whole = tokens.shape
    cap = 2 * tok_rows * TOPW // groups
    any_space = pl.BlockSpec(memory_space=pl.ANY)
    f32, bf16 = jnp.float32, jnp.bfloat16
    dma = pltpu.SemaphoreType.DMA
    mixed, _ = pl.pallas_call(
        layer_kernel,
        out_shape=(
            jax.ShapeDtypeStruct((tok_rows, width), bf16),
            jax.ShapeDtypeStruct((groups, tok_rows, whole), bf16),
        ),
        in_specs=[any_space] * 9,
        out_specs=(pl.BlockSpec(memory_space=pltpu.VMEM), any_space),
        scratch_shapes=[pltpu.VMEM((rows_in, wide), t) for t in (f32, f32, f32, bf16)]
        + [pltpu.VMEM((rows_out, width), t) for t in (f32, f32, f32, bf16)]
        + [
            pltpu.VMEM((2, dps * rows_in // 2, wide), bf16),
            pltpu.VMEM((dps * rows_out, width), bf16),
            pltpu.VMEM((2, tok_rows, whole), bf16),
            pltpu.VMEM((groups, tok_rows, whole - width), bf16),
            pltpu.VMEM((groups * cap, width), bf16),
            pltpu.VMEM((groups * cap, wide), f32),
            pltpu.VMEM((groups * cap, wide), bf16),
            pltpu.VMEM((ZN, groups * cap // ZN, width), bf16),
            pltpu.VMEM((ZN, 2 * YN * cap, width), bf16),
            pltpu.VMEM((ZN, 2, tok_rows, width), bf16),
            pltpu.VMEM((ZN, tok_rows, width), bf16),
            pltpu.VMEM((ZN, tok_rows, width), bf16),
            pltpu.VMEM((ZN - 1, tok_rows, width), bf16),
            dma((HALVES, 4)),
            dma((1,)),
            dma((7 * HALVES,)),
            dma((7 * HALVES,)),
            dma((34,)),
            dma((34,)),
            dma((2,)),
            dma((ZN, YN - 1)),
            dma((ZN, YN - 1)),
            dma((ZN,)),
            dma((ZN,)),
            dma((ZN - 1,)),
            dma((ZN - 1,)),
        ],
        name="moe_layer",
        compiler_params=pltpu.CompilerParams(
            collective_id=0, has_side_effects=True, vmem_limit_bytes=60 * 2**20
        ),
    )(tokens, w_in, m_in, v_in, g_in, w_out, m_out, v_out, g_out)
    return mixed


def per_device(tokens, routes, route_weight, w_in, m_in, v_in, g_in, w_out, m_out, v_out, g_out):
    tok_rows, width = tokens.shape
    two, depth, wide = w_in.shape[1:]
    whole = -(-(width + 3 * TOPW) // 128) * 128
    high = lax.reduce_precision(route_weight, 8, 7)
    low = route_weight - high
    packed = [tokens] + [a.astype(jnp.bfloat16) for a in (routes, high, low)]
    packed += [jnp.zeros((tok_rows, whole - width - 3 * TOPW), jnp.bfloat16)]
    return layer(
        jnp.concatenate(packed, axis=1),
        *(a.reshape(two * depth, wide) for a in (w_in, m_in, v_in, g_in)),
        *(a.reshape(a.shape[1:]) for a in (w_out, m_out, v_out, g_out)),
    )


def solution(mesh):
    placed = (
        P(("dp", "expert"), None),
        P(("dp", "expert"), None),
        P(("dp", "expert"), None),
        P("expert", None, "dp", None),
        P("expert", None, "dp", None),
        P("expert", None, "dp", None),
        P("expert", None, "dp", None),
        P("expert", "dp", None),
        P("expert", "dp", None),
        P("expert", "dp", None),
        P("expert", "dp", None),
    )
    return jax.shard_map(
        per_device, mesh=mesh, in_specs=placed, out_specs=P(("dp", "expert"), None), check_vma=False
    )
```

time: 294 us -> 231 us (0.79)
  Pallas kernels: 137 us -> 221 us
  waiting for transfers between devices: 79.7 us -> 0 us
  matrix products: 42.7 us -> 0 us
  starting transfers between devices: 19.7 us -> 0 us
    pallas_call x1, Pallas kernels: 137 us -> 221 us  [layer(): pl.pallas_call(layer_kernel, out_shape=(jax.ShapeDtypeStruct((tok_rows, w...]
    all_to_all x1 -> x0, waiting for transfers between devices: 79.7 us -> none  [per_device(): lax.all_to_all(results.reshape(groups, capacity, width), 'expert', split_...]
    dot_general x7 -> x0, matrix products: 42.7 us -> none  [the longest x1 16.4 us: per_device(): jnp.dot(hidden, down, preferred_element_type=jnp.float32)]
    all_to_all x1 -> x0, starting transfers between devices: 19.7 us -> none  [per_device(): lax.all_to_all(results.reshape(groups, capacity, width), 'expert', split_...]
    slice x1 -> x0, local copies, waits for them, and re-layouts: 4.16 us -> none  [per_device(): up_pre = jnp.dot(rows, gate_up[1], preferred_element_type=jnp.float32)]
  transfers between devices with their start and end apart: 1 -> 0, of which waited for: 1 -> 0; matrix products, arithmetic and copies ran while one was open for 0% -> 0% of each run, Pallas kernels for 0% -> 0%
where the time goes in v3:
time: 231 us; the launch traced here: 228 us
  Pallas kernels  221 us (96%)
  local copies, waits for them, and re-layouts  4.86 us (2%)
    pallas_call x1, Pallas kernels, layer(): pl.pallas_call(layer_kernel, out_shape=(jax.ShapeDtypeStruct((tok_rows, w...  221 us

profile of v3, /device:TPU:32, one launch (start us, length us, event | category | flops | bytes accessed | tf_op | source)
XLA Modules:
  0.0 227.7 jit_solution(16758014857992862146)
XLA Ops:
  0.0 0.7 convert_element_type.9
  0.7 0.7 fusion
  1.4 0.1 copy.17
  1.5 0.1 copy.18
  1.6 0.1 copy.16
  1.8 0.8 copy.15
  2.6 1.9 concatenate.3.tok
  4.4 221.5 %moe_layer.1 = (bf16[128,1792]{1,0:T(8,128)(2,1)}, bf16[32,128,1920]{2,1,0:T(8,128)(2,1)}) custom-call(bf16[128,1920]{1,0:T(8,128)(2,1)} %concatenate.3.tok, f32[448,1280]{1,0:T(8,128)} %bitcast.8, f32[448,1280]{1,0:T(8,128)} %bitcast.9, f32[448,1280]{1,0:T(8,128)} %bitcast.10, bf16[448,1280]{1,0:T(8,128)(2,1)} %bitcast.11, f32[160,1792]{1,0:T(8,128)} %bitcast.12, ...), custom_call_target="tpu_custom_call" | custom-call | tf_op jit(solution)/shard_map/moe_layer/pallas_call | solution.py:455
  225.9 1.8 copy.20
  (2 shorter events, 0.0 us)

commit v4 on v3

--- a/solution.py
+++ b/solution.py
@@ -15,7 +15,7 @@
 weight_decay = 0.1
 XN, YN, ZN = 4, 4, 4
 TOPW = 4
-HALVES = 6
+CHUNKS = 8
 
 
 def adamw(master, moment, second, gradient):
@@ -27,10 +27,10 @@
 
 
 def layer_kernel(
-    tok, w_in, m_in, v_in, g_in, w_out, m_out, v_out, g_out,
+    tokens, info_in, w_in, m_in, v_in, g_in, w_out, m_out, v_out, g_out,
     mixed, tok_all,
     wi, mi, vi, gi, wo, mo, vo, go, gu_v, dn_v,
-    tbuf, meta, rows_v, gate_v, hid_v, res_v, ry_v, part_v, sib_v, sum_v, zin_v,
+    tok, tbuf, meta, rows_v, gate_v, hid_v, res_v, ry_v, part_v, sib_v, sum_v, zin_v,
     load_sem, keep_sem, w_send, w_recv, t_send, t_recv, tin_sem, y_send, y_recv, s_send, s_recv, z_send, z_recv,
 ):
     d, e = lax.axis_index("dp"), lax.axis_index("expert")
@@ -42,20 +42,40 @@
     p_right, p_left, p_far = at_dp(1 - zh, x + 1), at_dp(1 - zh, x - 1), at_dp(1 - zh, x + 2)
     at_ex = lambda zz, yy, cc: lax.rem(zz + ZN, ZN) * (2 * YN) + lax.rem(yy + YN, YN) * 2 + cc
 
-    half_in, half_out = w_in.shape[0] // 4, w_out.shape[0] // 2
+    share_in, share_out = w_in.shape[0] // 2, w_out.shape[0]
+    half, third, rest = share_in // 2, share_out // 80 * 24, share_out // 80 * 16
+    pieces = [(0, 0, half), (0, half, half), (1, 0, half), (1, half, half)]
+    pieces += [(2, 0, third), (2, third, third), (2, 2 * third, rest), (2, 2 * third + rest, rest)]
+    tok_rows, width = tokens.shape
+    load_tok = pltpu.make_async_copy(tokens, tok.at[:, pl.ds(0, width)], keep_sem.at[1])
+    load_tok.start()
     loads = []
-    for h in range(HALVES):
+    for h, (kind, first, count) in enumerate(pieces):
         pairs = (
             ((w_in, wi), (m_in, mi), (v_in, vi), (g_in, gi))
-            if h < 4
+            if kind < 2
             else ((w_out, wo), (m_out, mo), (v_out, vo), (g_out, go))
         )
-        rows = pl.ds(h * half_in, half_in) if h < 4 else pl.ds((h - 4) * half_out, half_out)
+        rows = pl.ds(kind * share_in + first if kind < 2 else first, count)
         loads.append(
             [pltpu.make_async_copy(a.at[rows], b.at[rows], load_sem.at[h, i]) for i, (a, b) in enumerate(pairs)]
         )
         for cp in loads[h]:
             cp.start()
+    info = info_in[...]
+    info_high = info.astype(jnp.bfloat16).astype(jnp.float32)
+    info = jnp.concatenate(
+        [info_high, info - info_high, jnp.zeros((tok_rows - 2 * info.shape[0], tok_rows), jnp.float32)], axis=0
+    )
+    tok[:, width:] = info.T.astype(jnp.bfloat16)
+
+    @pl.when(z == 0)
+    def _():
+        zin_v[:ZN] = jnp.zeros((ZN,) + zin_v.shape[1:], zin_v.dtype)
+
+    @pl.when(z == ZN - 1)
+    def _():
+        zin_v[ZN:] = jnp.zeros((ZN,) + zin_v.shape[1:], zin_v.dtype)
 
     barrier = pltpu.get_barrier_semaphore()
     partners = [{"dp": p, "expert": e} for p in (right, left, mirror)]
@@ -87,6 +107,7 @@
             tok_copy(slot, at_ex(z, y + k, c), TY(b, k), src).start()
         tok_copy(slot, sibling, TS(b, 0), src).start()
 
+    load_tok.wait()
     own_tok = pltpu.make_async_copy(tok, tok_all.at[e], keep_sem.at[0])
     own_tok.start()
     can_up, can_down = z < ZN - 1, z > 0
@@ -140,11 +161,6 @@
             return
         pl.when(z >= n)(lambda: hand_on(z - n))
         pl.when(z < ZN - n)(lambda: hand_on(z + n))
-
-    def tok_arrive():
-        for b in range(ZN):
-            for k in range(YN):
-                tok_copy(at_ex(b, y - k, 1 - c), sibling, TS(b, k)).wait_recv()
 
     def tok_finish():
         for b in range(ZN):
@@ -163,14 +179,13 @@
                 tok_copy(e, sibling, DOWN(n)).wait_send()
 
     def slot_of(h, owner):
-        if h < 4:
-            first = pl.multiple_of(owner * (2 * half_in) + h % 2 * half_in, 16)
-            return gu_v.at[h // 2, pl.ds(first, half_in)]
-        first = pl.multiple_of(owner * (2 * half_out) + (h - 4) * half_out, 16)
-        return dn_v.at[pl.ds(first, half_out)]
+        kind, first, count = pieces[h]
+        if kind < 2:
+            return gu_v.at[kind, pl.ds(pl.multiple_of(owner * share_in + first, 16), count)]
+        return dn_v.at[pl.ds(pl.multiple_of(owner * share_out + first, 16), count)]
 
     def w_copy(h, owner, target, kind):
-        op = kind * HALVES + h
+        op = kind * CHUNKS + h
         return pltpu.make_async_remote_copy(
             src_ref=slot_of(h, owner), dst_ref=slot_of(h, owner),
             send_sem=w_send.at[op], recv_sem=w_recv.at[op],
@@ -187,15 +202,13 @@
     def w_wait(h, owner, kind):
         w_copy(h, owner, right, kind).wait_recv()
 
-    for h in range(HALVES):
+    for h in range(CHUNKS):
         for cp in loads[h]:
             cp.wait()
-        a, b, v, g, out, count, first = (
-            (wi, mi, vi, gi, gu_v.at[h // 2], half_in, h * half_in)
-            if h < 4
-            else (wo, mo, vo, go, dn_v, half_out, (h - 4) * half_out)
-        )
-        base = d * (2 * half_in) + h % 2 * half_in if h < 4 else d * (2 * half_out) + (h - 4) * half_out
+        kind, start, count = pieces[h]
+        a, b, v, g, out = (wi, mi, vi, gi, gu_v.at[kind]) if kind < 2 else (wo, mo, vo, go, dn_v)
+        first = kind * share_in + start if kind < 2 else start
+        base = d * (share_in if kind < 2 else share_out) + start
 
         def step(i, _, a=a, b=b, v=v, g=g, out=out, first=first, base=base):
             at = pl.ds(pl.multiple_of(first + i * 16, 16), 16)
@@ -233,8 +246,7 @@
         else:
             w_send_to(h, p_right, left, F_P)
 
-    width, wide = dn_v.shape[1], dn_v.shape[0]
-    tok_rows = tok.shape[0]
+    wide = dn_v.shape[0]
     blocks = tok_all.shape[0]
     cap = rows_v.shape[0] // blocks
     f32, bf16 = jnp.float32, jnp.bfloat16
@@ -249,25 +261,33 @@
         for k in range(TOPW):
             same = info[:, k : k + 1] == expert
             hit = jnp.where(same, 1.0, hit)
-            share = info[:, TOPW + k : TOPW + k + 1] + info[:, 2 * TOPW + k : 2 * TOPW + k + 1]
+            share = info[:, TOPW + k : TOPW + k + 1] + info[:, 3 * TOPW + k : 3 * TOPW + k + 1]
             weight = jnp.where(same, share, weight)
         earlier = (iota((tok_rows, tok_rows), 1) < iota((tok_rows, tok_rows), 0)).astype(bf16)
         rank = jnp.dot(earlier, hit.astype(bf16), preferred_element_type=f32)
         return jnp.logical_and(rank == slot, hit > 0.0), weight
 
+    DEEP = 4
+
     def tok_in(s):
-        return pltpu.make_async_copy(tok_all.at[s], tbuf.at[lax.rem(s, 2)], tin_sem.at[lax.rem(s, 2)])
-
-    def pick_rows():
-        tok_in(0).start()
-
-        def step(s, _):
-            @pl.when(s < blocks - 1)
+        return pltpu.make_async_copy(tok_all.at[s], tbuf.at[lax.rem(s, DEEP)], tin_sem.at[lax.rem(s, DEEP)])
+
+    def pick_rows(b):
+        per = 2 * YN
+        for k in range(YN):
+            tok_copy(at_ex(b, y - k, 1 - c), sibling, TS(b, k)).wait_recv()
+        for i in range(DEEP - 1):
+            tok_in(b * per + i).start()
+
+        def step(i, _):
+            s = b * per + i
+
+            @pl.when(i < per - DEEP + 1)
             def _():
-                tok_in(s + 1).start()
+                tok_in(s + DEEP - 1).start()
 
             tok_in(s).wait()
-            at = lax.rem(s, 2)
+            at = lax.rem(s, DEEP)
             info = tbuf[at, :, width:]
             meta[s] = info
             ours = jnp.zeros((1, cap), f32) + e.astype(f32)
@@ -279,7 +299,7 @@
             rows_v[pl.ds(pl.multiple_of(s * cap, cap), cap), :] = picked.astype(bf16)
             return 0
 
-        lax.fori_loop(0, blocks, step, 0)
+        lax.fori_loop(0, per, step, 0)
 
     tall, tile = 512, 256
 
@@ -325,10 +345,11 @@
             device_id={"dp": d, "expert": sibling}, device_id_type=MESH,
         )
 
-    def z_copy(j, zt):
+    def z_copy(zt, up):
+        slot = jnp.where(up, zt, ZN + zt)
         return pltpu.make_async_remote_copy(
-            src_ref=sum_v.at[zt], dst_ref=zin_v.at[j - 1], send_sem=z_send.at[j - 1], recv_sem=z_recv.at[j - 1],
-            device_id={"dp": d, "expert": at_ex(zt, y, c)}, device_id_type=MESH,
+            src_ref=sum_v.at[zt], dst_ref=zin_v.at[slot], send_sem=z_send.at[slot], recv_sem=z_recv.at[slot],
+            device_id={"dp": d, "expert": at_ex(jnp.where(up, z + 1, z - 1), y, c)}, device_id_type=MESH,
         )
 
     def partial(i, zt):
@@ -357,97 +378,114 @@
         lax.fori_loop(0, width // tile, step, 0)
         s_copy(i, zt).start()
 
-    def both_cores(i, zt):
+    def both_cores(i, zt, on):
         s_copy(i, zt).wait_recv()
+        up = zt > z
+        slot = jnp.where(up, zt, ZN + zt)
+        if on:
+
+            @pl.when(jnp.where(up, z, ZN - 1 - z) > 0)
+            def _():
+                z_copy(zt, up).wait_recv()
 
         def step(n, _):
             at = pl.ds(pl.multiple_of(n * 16, 16), 16)
-            sum_v[zt, at, :] = (part_v[zt, c, at, :].astype(f32) + sib_v[zt, at, :].astype(f32)).astype(bf16)
+            total = part_v[zt, c, at, :].astype(f32) + sib_v[zt, at, :].astype(f32)
+            if on:
+                sum_v[zt, at, :] = (total + zin_v[slot, at, :].astype(f32)).astype(bf16)
+            else:
+                mixed[at, :] = (total + zin_v[z, at, :].astype(f32) + zin_v[ZN + z, at, :].astype(f32)).astype(bf16)
             return 0
 
+        if not on:
+            pl.when(z > 0)(lambda: z_copy(z, True).wait_recv())
+            pl.when(z < ZN - 1)(lambda: z_copy(z, False).wait_recv())
         lax.fori_loop(0, tok_rows // 16, step, 0)
+        if on:
+            z_copy(zt, up).start()
+
+    def gate_up_arrive(*some):
+        for h in some:
+            w_wait(h, far, F_OWN)
+            w_wait(h, p_far, F_P)
 
     tok_z(1)
     fwd_own(0)
     fwd_own(1)
-    to_mirror(2)
     tok_z(2)
     fwd_own(2)
     fwd_own(3)
+    from_mirror(0)
+    to_mirror(2)
+    tok_z(3)
+    for h in range(4, CHUNKS):
+        fwd_own(h)
+    from_mirror(1)
     to_mirror(3)
-    tok_z(3)
-    fwd_own(4)
-    fwd_own(5)
-    from_mirror(0)
-    to_mirror(4)
+    fwd_mirror(0)
     tok_y(0)
-    from_mirror(1)
-    fwd_mirror(0)
-    to_mirror(5)
     tok_y(1)
     from_mirror(2)
+    to_mirror(4)
     fwd_mirror(1)
     tok_y(2)
     tok_y(3)
+    own_tok.wait()
+    pick_rows(0)
     from_mirror(3)
+    to_mirror(5)
     fwd_mirror(2)
-    own_tok.wait()
-    tok_arrive()
-    pick_rows()
+    pick_rows(1)
     from_mirror(4)
+    to_mirror(6)
+    pick_rows(2)
     fwd_mirror(3)
-    for h in (0, 1):
-        w_wait(h, far, F_OWN)
-        w_wait(h, p_far, F_P)
+    from_mirror(5)
+    to_mirror(7)
+    pick_rows(3)
+    fwd_mirror(4)
+    from_mirror(6)
+    fwd_mirror(5)
+    from_mirror(7)
+    gate_up_arrive(0, 1)
     up_tiles(False)
-    from_mirror(5)
-    fwd_mirror(4)
-    fwd_mirror(5)
-    for h in (2, 3):
-        w_wait(h, far, F_OWN)
-        w_wait(h, p_far, F_P)
+    fwd_mirror(6)
+    fwd_mirror(7)
+    gate_up_arrive(2, 3)
     up_tiles(True)
-    for h in (4, 5):
-        w_wait(h, far, F_OWN)
-        w_wait(h, p_far, F_P)
-    order = [(i, j, lax.rem(z + j, ZN)) for i, j in enumerate((2, 1, 3, 0))]
-    for i, j, zt in order:
+    gate_up_arrive(4, 5, 6, 7)
+
+    def by_z(*table):
+        out = jnp.int32(table[-1])
+        for at in range(ZN - 1):
+            out = jnp.where(z == at, table[at], out)
+        return out
+
+    order = list(enumerate((by_z(3, 3, 0, 0), by_z(2, 0, 3, 1), by_z(1, 2, 1, 2), z)))
+    for i, zt in order:
         down(i, zt)
-    for i, j, zt in order:
+    for i, zt in order:
         partial(i, zt)
-        both_cores(i, zt)
-        if j:
-            z_copy(j, zt).start()
-    for j in range(1, ZN):
-        z_copy(j, z).wait_recv()
-
-    def step(n, _):
-        at = pl.ds(pl.multiple_of(n * 16, 16), 16)
-        total = sum_v[z, at, :].astype(f32)
-        for j in range(ZN - 1):
-            total = total + zin_v[j, at, :].astype(f32)
-        mixed[at, :] = total.astype(bf16)
-        return 0
-
-    lax.fori_loop(0, tok_rows // 16, step, 0)
-    for i, j, zt in order:
+        both_cores(i, zt, i < ZN - 1)
+    for i, zt in order:
         for k in range(1, YN):
             y_copy(i, zt, k, lax.rem(y + k, YN)).wait_send()
         s_copy(i, zt).wait_send()
-        if j:
-            z_copy(j, zt).wait_send()
-    for h in (4, 5):
+        if i < ZN - 1:
+            z_copy(zt, zt > z).wait_send()
+    for h in (CHUNKS - 2, CHUNKS - 1):
         w_copy(h, d, mirror, MIR).wait_send()
     tok_finish()
     for cp in sent:
         cp.wait_send()
 
 
-def layer(tokens, w_in, m_in, v_in, g_in, w_out, m_out, v_out, g_out):
+def layer(tokens, info, w_in, m_in, v_in, g_in, w_out, m_out, v_out, g_out):
     rows_in, wide = w_in.shape
     rows_out, width = w_out.shape
     groups, dps = lax.axis_size("expert"), lax.axis_size("dp")
-    tok_rows, whole = tokens.shape
+    tok_rows = tokens.shape[0]
+    whole = width + 128
     cap = 2 * tok_rows * TOPW // groups
     any_space = pl.BlockSpec(memory_space=pl.ANY)
     f32, bf16 = jnp.float32, jnp.bfloat16
@@ -458,14 +496,15 @@
             jax.ShapeDtypeStruct((tok_rows, width), bf16),
             jax.ShapeDtypeStruct((groups, tok_rows, whole), bf16),
         ),
-        in_specs=[any_space] * 9,
+        in_specs=[any_space, pl.BlockSpec(memory_space=pltpu.VMEM)] + [any_space] * 8,
         out_specs=(pl.BlockSpec(memory_space=pltpu.VMEM), any_space),
         scratch_shapes=[pltpu.VMEM((rows_in, wide), t) for t in (f32, f32, f32, bf16)]
         + [pltpu.VMEM((rows_out, width), t) for t in (f32, f32, f32, bf16)]
         + [
             pltpu.VMEM((2, dps * rows_in // 2, wide), bf16),
             pltpu.VMEM((dps * rows_out, width), bf16),
-            pltpu.VMEM((2, tok_rows, whole), bf16),
+            pltpu.VMEM((tok_rows, whole), bf16),
+            pltpu.VMEM((4, tok_rows, whole), bf16),
             pltpu.VMEM((groups, tok_rows, whole - width), bf16),
             pltpu.VMEM((groups * cap, width), bf16),
             pltpu.VMEM((groups * cap, wide), f32),
@@ -475,39 +514,34 @@
             pltpu.VMEM((ZN, 2, tok_rows, width), bf16),
             pltpu.VMEM((ZN, tok_rows, width), bf16),
             pltpu.VMEM((ZN, tok_rows, width), bf16),
-            pltpu.VMEM((ZN - 1, tok_rows, width), bf16),
-            dma((HALVES, 4)),
-            dma((1,)),
-            dma((7 * HALVES,)),
-            dma((7 * HALVES,)),
+            pltpu.VMEM((2 * ZN, tok_rows, width), bf16),
+            dma((CHUNKS, 4)),
+            dma((2,)),
+            dma((7 * CHUNKS,)),
+            dma((7 * CHUNKS,)),
             dma((34,)),
             dma((34,)),
-            dma((2,)),
+            dma((4,)),
             dma((ZN, YN - 1)),
             dma((ZN, YN - 1)),
             dma((ZN,)),
             dma((ZN,)),
-            dma((ZN - 1,)),
-            dma((ZN - 1,)),
+            dma((2 * ZN,)),
+            dma((2 * ZN,)),
         ],
         name="moe_layer",
         compiler_params=pltpu.CompilerParams(
             collective_id=0, has_side_effects=True, vmem_limit_bytes=60 * 2**20
         ),
-    )(tokens, w_in, m_in, v_in, g_in, w_out, m_out, v_out, g_out)
+    )(tokens, info, w_in, m_in, v_in, g_in, w_out, m_out, v_out, g_out)
     return mixed
 
 
 def per_device(tokens, routes, route_weight, w_in, m_in, v_in, g_in, w_out, m_out, v_out, g_out):
-    tok_rows, width = tokens.shape
     two, depth, wide = w_in.shape[1:]
-    whole = -(-(width + 3 * TOPW) // 128) * 128
-    high = lax.reduce_precision(route_weight, 8, 7)
-    low = route_weight - high
-    packed = [tokens] + [a.astype(jnp.bfloat16) for a in (routes, high, low)]
-    packed += [jnp.zeros((tok_rows, whole - width - 3 * TOPW), jnp.bfloat16)]
     return layer(
-        jnp.concatenate(packed, axis=1),
+        tokens,
+        jnp.concatenate([routes.T.astype(jnp.float32), route_weight.T], axis=0),
         *(a.reshape(two * depth, wide) for a in (w_in, m_in, v_in, g_in)),
         *(a.reshape(a.shape[1:]) for a in (w_out, m_out, v_out, g_out)),
     )

time: 231 us -> 207 us (0.90); the launches traced: 228 us -> 207 us
  Pallas kernels: 221 us -> 203 us
  local copies, waits for them, and re-layouts: 4.86 us -> 1.82 us
    pallas_call x1, Pallas kernels: 221 us -> 203 us  [layer(): pl.pallas_call(layer_kernel, out_shape=(jax.ShapeDtypeStruct((tok_rows, w...]
where the time goes in v4:
time: 207 us
  Pallas kernels  203 us (98%)
    pallas_call x1, Pallas kernels, layer(): pl.pallas_call(layer_kernel, out_shape=(jax.ShapeDtypeStruct((tok_rows, w...  203 us

profile of v4, /device:TPU:32, one launch (start us, length us, event | category | flops | bytes accessed | tf_op | source)
XLA Modules:
  0.0 207.2 jit_solution(13975243042950903635)
XLA Ops:
  0.0 0.7 convert_bitcast_fusion
  0.7 1.3 pad_maximum_fusion.info_in
  2.0 203.4 %moe_layer.1 = (bf16[128,1792]{1,0:T(8,128)(2,1)}, bf16[32,128,1920]{2,1,0:T(8,128)(2,1)}) custom-call(bf16[128,1792]{1,0:T(8,128)(2,1)} %tokens.1, f32[8,128]{1,0:T(8,128)} %pad_maximum_fusion.info_in, f32[448,1280]{1,0:T(8,128)} %bitcast.11, f32[448,1280]{1,0:T(8,128)} %bitcast.12, f32[448,1280]{1,0:T(8,128)} %bitcast.13, bf16[448,1280]{1,0:T(8,128)(2,1)} %bitcast.14, ...), custom_call_target="tpu_custom_call" | custom-call | tf_op jit(solution)/shard_map/moe_layer/pallas_call | solution.py:493
  205.4 1.8 copy.13

commit v5 on v4

--- a/solution.py
+++ b/solution.py
@@ -345,27 +345,37 @@
             device_id={"dp": d, "expert": sibling}, device_id_type=MESH,
         )
 
-    def z_copy(zt, up):
+    part_rows = tok_rows // 2
+
+    def z_copy(zt, up, part):
         slot = jnp.where(up, zt, ZN + zt)
+        rows = pl.ds(part * part_rows, part_rows)
         return pltpu.make_async_remote_copy(
-            src_ref=sum_v.at[zt], dst_ref=zin_v.at[slot], send_sem=z_send.at[slot], recv_sem=z_recv.at[slot],
+            src_ref=sum_v.at[zt, rows], dst_ref=zin_v.at[slot, rows],
+            send_sem=z_send.at[slot, part], recv_sem=z_recv.at[slot, part],
             device_id={"dp": d, "expert": at_ex(jnp.where(up, z + 1, z - 1), y, c)}, device_id_type=MESH,
         )
+
+    def spread_rows(i, zt):
+        lane = iota((1, YN * pair), 1)
+        expert = (z * (2 * YN) + lane // pair * 2 + c).astype(f32)
+        slot = lax.rem(lane, cap).astype(f32)
+        for cc in range(2):
+            place, weight = routed(meta[zt * (2 * YN) + y * 2 + cc].astype(f32), expert, slot)
+            place = jnp.logical_and(place, lax.rem(lane // cap, 2) == cc)
+            spread = jnp.where(place, weight, 0.0)
+            high = spread.astype(bf16)
+            first = cc * 2 * lane.shape[1]
+            tbuf[i, :, first : first + lane.shape[1]] = high
+            tbuf[i, :, first + lane.shape[1] : first + 2 * lane.shape[1]] = (spread - high.astype(f32)).astype(bf16)
 
     def partial(i, zt):
         for k in range(1, YN):
             y_copy(i, zt, k, y).wait_recv()
-        lane = iota((1, YN * pair), 1)
-        expert = (z * (2 * YN) + lane // pair * 2 + c).astype(f32)
-        slot = lax.rem(lane, cap).astype(f32)
-        spread = []
-        for cc in range(2):
-            place, weight = routed(meta[zt * (2 * YN) + y * 2 + cc].astype(f32), expert, slot)
-            place = jnp.logical_and(place, lax.rem(lane // cap, 2) == cc)
-            spread.append(jnp.where(place, weight, 0.0))
-        spread = jnp.concatenate(spread, axis=0)
-        high = spread.astype(bf16)
-        low = (spread - high.astype(f32)).astype(bf16)
+        lanes = YN * pair
+        high, low = (
+            jnp.concatenate([tbuf[i, :, f * lanes : (f + 1) * lanes] for f in (at, at + 2)], axis=0) for at in range(2)
+        )
 
         def step(n, _):
             cols = pl.ds(pl.multiple_of(n * tile, tile), tile)
@@ -382,27 +392,29 @@
         s_copy(i, zt).wait_recv()
         up = zt > z
         slot = jnp.where(up, zt, ZN + zt)
-        if on:
-
-            @pl.when(jnp.where(up, z, ZN - 1 - z) > 0)
-            def _():
-                z_copy(zt, up).wait_recv()
-
-        def step(n, _):
-            at = pl.ds(pl.multiple_of(n * 16, 16), 16)
-            total = part_v[zt, c, at, :].astype(f32) + sib_v[zt, at, :].astype(f32)
+        for part in range(2):
             if on:
-                sum_v[zt, at, :] = (total + zin_v[slot, at, :].astype(f32)).astype(bf16)
+
+                @pl.when(jnp.where(up, z, ZN - 1 - z) > 0)
+                def _():
+                    z_copy(zt, up, part).wait_recv()
+
             else:
-                mixed[at, :] = (total + zin_v[z, at, :].astype(f32) + zin_v[ZN + z, at, :].astype(f32)).astype(bf16)
-            return 0
-
-        if not on:
-            pl.when(z > 0)(lambda: z_copy(z, True).wait_recv())
-            pl.when(z < ZN - 1)(lambda: z_copy(z, False).wait_recv())
-        lax.fori_loop(0, tok_rows // 16, step, 0)
-        if on:
-            z_copy(zt, up).start()
+                pl.when(z > 0)(lambda: z_copy(z, True, part).wait_recv())
+                pl.when(z < ZN - 1)(lambda: z_copy(z, False, part).wait_recv())
+
+            def step(n, _):
+                at = pl.ds(pl.multiple_of(part * part_rows + n * 16, 16), 16)
+                total = part_v[zt, c, at, :].astype(f32) + sib_v[zt, at, :].astype(f32)
+                if on:
+                    sum_v[zt, at, :] = (total + zin_v[slot, at, :].astype(f32)).astype(bf16)
+                else:
+                    mixed[at, :] = (total + zin_v[z, at, :].astype(f32) + zin_v[ZN + z, at, :].astype(f32)).astype(bf16)
+                return 0
+
+            lax.fori_loop(0, part_rows // 16, step, 0)
+            if on:
+                z_copy(zt, up, part).start()
 
     def gate_up_arrive(*some):
         for h in some:
@@ -465,6 +477,8 @@
     for i, zt in order:
         down(i, zt)
     for i, zt in order:
+        spread_rows(i, zt)
+    for i, zt in order:
         partial(i, zt)
         both_cores(i, zt, i < ZN - 1)
     for i, zt in order:
@@ -472,7 +486,8 @@
             y_copy(i, zt, k, lax.rem(y + k, YN)).wait_send()
         s_copy(i, zt).wait_send()
         if i < ZN - 1:
-            z_copy(zt, zt > z).wait_send()
+            for part in range(2):
+                z_copy(zt, zt > z, part).wait_send()
     for h in (CHUNKS - 2, CHUNKS - 1):
         w_copy(h, d, mirror, MIR).wait_send()
     tok_finish()
@@ -526,12 +541,12 @@
             dma((ZN, YN - 1)),
             dma((ZN,)),
             dma((ZN,)),
-            dma((2 * ZN,)),
-            dma((2 * ZN,)),
+            dma((2 * ZN, 2)),
+            dma((2 * ZN, 2)),
         ],
         name="moe_layer",
         compiler_params=pltpu.CompilerParams(
-            collective_id=0, has_side_effects=True, vmem_limit_bytes=60 * 2**20
+            collective_id=0, has_side_effects=True, vmem_limit_bytes=62 * 2**20
         ),
     )(tokens, info, w_in, m_in, v_in, g_in, w_out, m_out, v_out, g_out)
     return mixed

time: 207 us -> 201 us (0.971)
  Pallas kernels: 203 us -> 197 us
    pallas_call x1, Pallas kernels: 203 us -> 197 us  [layer(): pl.pallas_call(layer_kernel, out_shape=(jax.ShapeDtypeStruct((tok_rows, w...]
where the time goes in v5:
time: 201 us
  Pallas kernels  197 us (98%)
    pallas_call x1, Pallas kernels, layer(): pl.pallas_call(layer_kernel, out_shape=(jax.ShapeDtypeStruct((tok_rows, w...  197 us

profile of v5, /device:TPU:32, one launch (start us, length us, event | category | flops | bytes accessed | tf_op | source)
XLA Modules:
  0.0 200.6 jit_solution(16002127150381262732)
XLA Ops:
  0.0 0.7 convert_bitcast_fusion
  0.7 1.3 pad_maximum_fusion.info_in
  2.0 196.8 %moe_layer.1 = (bf16[128,1792]{1,0:T(8,128)(2,1)}, bf16[32,128,1920]{2,1,0:T(8,128)(2,1)}) custom-call(bf16[128,1792]{1,0:T(8,128)(2,1)} %tokens.1, f32[8,128]{1,0:T(8,128)} %pad_maximum_fusion.info_in, f32[448,1280]{1,0:T(8,128)} %bitcast.11, f32[448,1280]{1,0:T(8,128)} %bitcast.12, f32[448,1280]{1,0:T(8,128)} %bitcast.13, bf16[448,1280]{1,0:T(8,128)(2,1)} %bitcast.14, ...), custom_call_target="tpu_custom_call" | custom-call | tf_op jit(solution)/shard_map/moe_layer/pallas_call | solution.py:508
  198.7 1.8 copy.13

commit v6 on v5

--- a/solution.py
+++ b/solution.py
@@ -345,7 +345,7 @@
             device_id={"dp": d, "expert": sibling}, device_id_type=MESH,
         )
 
-    part_rows = tok_rows // 2
+    part_rows = tok_rows // 4
 
     def z_copy(zt, up, part):
         slot = jnp.where(up, zt, ZN + zt)
@@ -392,7 +392,7 @@
         s_copy(i, zt).wait_recv()
         up = zt > z
         slot = jnp.where(up, zt, ZN + zt)
-        for part in range(2):
+        for part in range(4):
             if on:
 
                 @pl.when(jnp.where(up, z, ZN - 1 - z) > 0)
@@ -486,7 +486,7 @@
             y_copy(i, zt, k, lax.rem(y + k, YN)).wait_send()
         s_copy(i, zt).wait_send()
         if i < ZN - 1:
-            for part in range(2):
+            for part in range(4):
                 z_copy(zt, zt > z, part).wait_send()
     for h in (CHUNKS - 2, CHUNKS - 1):
         w_copy(h, d, mirror, MIR).wait_send()
@@ -541,8 +541,8 @@
             dma((ZN, YN - 1)),
             dma((ZN,)),
             dma((ZN,)),
-            dma((2 * ZN, 2)),
-            dma((2 * ZN, 2)),
+            dma((2 * ZN, 4)),
+            dma((2 * ZN, 4)),
         ],
         name="moe_layer",
         compiler_params=pltpu.CompilerParams(

time: 201 us -> 200 us (level)
    pallas_call x1, Pallas kernels: 197 us -> 195 us  [layer(): pl.pallas_call(layer_kernel, out_shape=(jax.ShapeDtypeStruct((tok_rows, w...]
where the time goes in v6:
time: 200 us; the launch traced here: 199 us
  Pallas kernels  195 us (98%)
    pallas_call x1, Pallas kernels, layer(): pl.pallas_call(layer_kernel, out_shape=(jax.ShapeDtypeStruct((tok_rows, w...  195 us

profile of v6, /device:TPU:32, one launch (start us, length us, event | category | flops | bytes accessed | tf_op | source)
XLA Modules:
  0.0 198.5 jit_solution(13993806038625104422)
XLA Ops:
  0.0 0.7 convert_bitcast_fusion
  0.7 1.3 pad_maximum_fusion.info_in
  2.0 194.8 %moe_layer.1 = (bf16[128,1792]{1,0:T(8,128)(2,1)}, bf16[32,128,1920]{2,1,0:T(8,128)(2,1)}) custom-call(bf16[128,1792]{1,0:T(8,128)(2,1)} %tokens.1, f32[8,128]{1,0:T(8,128)} %pad_maximum_fusion.info_in, f32[448,1280]{1,0:T(8,128)} %bitcast.11, f32[448,1280]{1,0:T(8,128)} %bitcast.12, f32[448,1280]{1,0:T(8,128)} %bitcast.13, bf16[448,1280]{1,0:T(8,128)(2,1)} %bitcast.14, ...), custom_call_target="tpu_custom_call" | custom-call | tf_op jit(solution)/shard_map/moe_layer/pallas_call | solution.py:508
  196.7 1.8 copy.13
